TPU v7x, 32 devices: a whole 2x2x4 slice. The times are simulated.
32 devices in a mesh: ctx: 16 (over z, x, core), head: 2 (over y).
Axes of the slice: x: 2, y: 2, z: 4, core: 2. Of those that a mesh axis runs over, the one named last changes fastest.
Arguments:
- queries: bfloat16 [3072, 6144], P(('ctx', 'head')), may hold values from -9 to 9
- noisy_token_keys: bfloat16 [3072, 1024], P(('ctx', 'head')), may hold values from -9 to 9
- noisy_token_values: bfloat16 [3072, 1024], P(('ctx', 'head')), may hold values from -6 to 6
- clean_token_keys: bfloat16 [1024, 1024], P(('ctx', 'head')), may hold values from -9 to 9
- clean_token_values: bfloat16 [1024, 1024], P(('ctx', 'head')), may hold values from -6 to 6
- output_gradient: bfloat16 [3072, 6144], P(('ctx', 'head')), may hold values from -6 to 6
- history_list: int32 [16, 16], replicated, may hold values from -1 to 1, as said below
Outputs:
- attn_out: bfloat16 [3072, 6144], P(('ctx', 'head'))
- grad_query: bfloat16 [3072, 6144], P(('ctx', 'head'))
- noisy_key_gradient: bfloat16 [3072, 1024], P(('ctx', 'head'))
- noisy_value_gradient: bfloat16 [3072, 1024], P(('ctx', 'head'))
- grad_key_clean: bfloat16 [1024, 1024], P(('ctx', 'head'))
- grad_value_clean: bfloat16 [1024, 1024], P(('ctx', 'head'))
Inputs may be any that keep to these rules, and one draw needn't show every extreme that they name: history_list[d, s] is -1 or a block number below 2; it is -1 unless floor(s / 2) < floor(d / 2); each row has at most 14 entries that are not -1, and some row has exactly 14.
All inputs are finite; a program needn't handle non-finite values.
Results may differ from a plain program's by a relative error of at most 0.018.
Values may be sent and summed in bfloat16 or wider, within the bound.
No kernel may reach another device: no remote copies, remote signals or barrier semaphores. Data moves between devices by JAX's collectives and lax.ppermute only.
A program may use at most 64 MiB of HBM per device.

v0:
```python
import functools

import jax
import jax.numpy as jnp
from jax import lax
from jax.experimental import pallas as pl
from jax.experimental.pallas import tpu as pltpu
from jax.sharding import PartitionSpec as P

QUERY_HEADS = 48
KEY_VALUE_HEADS = 8
HEAD_SIZE = 128
BLK = 32
HEADS_PER_GROUP = QUERY_HEADS // KEY_VALUE_HEADS
GROUP_WIDTH = HEADS_PER_GROUP * HEAD_SIZE
SCALE = HEAD_SIZE**-0.5
LOG2E = 1.4426950408889634

NEG_FILL = -1e30
SLICE_ROWS = 256
KERNEL_VMEM = 32 * 2**20


def flipped(block, bits):
    count = lax.axis_size("ctx")
    return lax.ppermute(block, "ctx", [(i, i ^ bits) for i in range(count)])


def shifted(block, step):
    count = lax.axis_size("head")
    return lax.ppermute(block, "head", [(i, (i + step) % count) for i in range(count)])


def dot(a, b, contract):
    return lax.dot_general(
        a, b, ((contract[:1], contract[1:]), ((), ())), preferred_element_type=jnp.float32
    )


def lanes(start, size):
    return pl.ds(pl.multiple_of(start, HEAD_SIZE), size)


def pack_kernel(head_count, groups, k_noisy, v_noisy, k_clean, v_clean, *outs):
    rows = k_noisy.shape[0]
    half = k_noisy.shape[1] // head_count
    width = HEAD_SIZE
    for index, group in enumerate(groups):
        for step in range(head_count):
            out = outs[index * head_count + step]
            target = lax.rem(lax.axis_index("head") + step, head_count)
            for at, member in enumerate(group):
                source = lanes(target * half + member * width, width)
                for n, (noisy, clean) in enumerate(((k_noisy, k_clean), (v_noisy, v_clean))):
                    to = slice((2 * at + n) * width, (2 * at + n + 1) * width)
                    out[:rows, to] = noisy[:, source]
                    out[rows:, to] = clean[:, source]


def packed(head_count, groups, k_noisy, v_noisy, k_clean, v_clean):
    vmem = pl.BlockSpec(memory_space=pltpu.VMEM)
    rows = k_noisy.shape[0] + k_clean.shape[0]
    shapes = [
        jax.ShapeDtypeStruct((rows, 2 * HEAD_SIZE * len(group)), jnp.bfloat16)
        for group in groups
        for _ in range(head_count)
    ]
    outs = pl.pallas_call(
        functools.partial(pack_kernel, head_count, groups),
        in_specs=[vmem] * 4,
        out_specs=[vmem] * len(shapes),
        out_shape=shapes,
        name="pack_keys_values",
    )(k_noisy, v_noisy, k_clean, v_clean)
    return [outs[i * head_count : (i + 1) * head_count] for i in range(len(groups))]


def stack_kernel(head_count, q, g, *outs):
    rows = q.shape[0]
    per_device = KEY_VALUE_HEADS // head_count
    for member in range(per_device):
        for step in range(head_count):
            out = outs[member * head_count + step]
            target = lax.rem(lax.axis_index("head") + step, head_count)
            source = lanes((target * per_device + member) * GROUP_WIDTH, GROUP_WIDTH)
            out[:rows, :] = q[:, source]
            out[rows:, :] = g[:, source]


def query_blocks(head_count, q, g):
    vmem = pl.BlockSpec(memory_space=pltpu.VMEM)
    shape = jax.ShapeDtypeStruct((2 * q.shape[0], GROUP_WIDTH), jnp.bfloat16)
    outs = pl.pallas_call(
        functools.partial(stack_kernel, head_count),
        in_specs=[vmem] * 2,
        out_specs=[vmem] * KEY_VALUE_HEADS,
        out_shape=[shape] * KEY_VALUE_HEADS,
        name="stack_queries",
    )(q, g)
    return [outs[i : i + head_count] for i in range(0, KEY_VALUE_HEADS, head_count)]


def attention_kernel(shape, column, kept, listed, place, own, *refs):
    head_count, group_rows, store_rows, clean_rows, slots = shape
    received, refs = refs[: head_count - 1], refs[head_count - 1 :]
    near, far, *refs = refs
    o_all, gq_all, *refs = refs[kept:]
    sends, refs = refs[: head_count - 1], refs[head_count - 1 :]
    near_grad, far_grad, k_all, v_all, q_all, g_all, o_out, gq_out, o_own, gq_own, copied = refs
    rows = own.shape[0] // 2
    width = HEAD_SIZE
    position, head = place[0], place[1]
    k_cols = slice(2 * column * width, (2 * column + 1) * width)
    v_cols = slice((2 * column + 1) * width, (2 * column + 2) * width)
    depth = (near.shape[0] - group_rows) // (2 * store_rows)

    def placed(slot):
        apart = lax.bitwise_xor(position, slot)
        store = lax.bitwise_and(lax.shift_right_logical(apart, 1), 1) * depth
        store = store + lax.shift_right_logical(apart, 2)
        block = jnp.maximum(listed[position, slot], 0)
        if clean_rows >= BLK:
            owner = lax.div(block * BLK, clean_rows)
            step = lax.rem(head - owner + head_count, head_count)
            inside = step * clean_rows + block * BLK - owner * clean_rows
        else:
            inside = block * BLK
        start = pl.multiple_of(group_rows + store * store_rows + inside, BLK)
        return lax.bitwise_and(apart, 1), pl.ds(start, BLK)

    k_all[:group_rows, :] = near[:group_rows, k_cols]
    v_all[:group_rows, :] = near[:group_rows, v_cols]
    k_all[group_rows : 2 * group_rows, :] = far[:group_rows, k_cols]
    v_all[group_rows : 2 * group_rows, :] = far[:group_rows, v_cols]
    span = 2 * group_rows
    total = span + slots * BLK
    for slot in range(slots):
        other, source = placed(slot)
        to = slice(span + slot * BLK, span + (slot + 1) * BLK)
        k_all[to, :] = jnp.where(other == 1, far[source, k_cols], near[source, k_cols])
        v_all[to, :] = jnp.where(other == 1, far[source, v_cols], near[source, v_cols])
    at = 0
    for r in range(HEADS_PER_GROUP):
        for part in (own, *received):
            q_all[at : at + rows, :] = part[:rows, r * width : (r + 1) * width]
            g_all[at : at + rows, :] = part[rows:, r * width : (r + 1) * width]
            at += rows

    keys = k_all[...]
    values = v_all[...]
    keys_t = keys.T
    values_t = values.T
    biases = [
        jnp.where(listed[position, slot] >= 0, 0.0, NEG_FILL).astype(jnp.float32)
        for slot in range(slots)
    ]
    cuts = list(range(0, at - SLICE_ROWS + 1, SLICE_ROWS)) + [at]
    slices = [slice(low, high) for low, high in zip(cuts, cuts[1:])]

    def products(piece):
        query, upstream = q_all[piece, :], g_all[piece, :]
        return query, upstream, dot(keys, query, (1, 1)), dot(values, upstream, (1, 1))

    def softmax(scores, dprob):
        scores = scores * (SCALE * LOG2E)
        pieces = [scores[:span]]
        for slot in range(slots):
            low = span + slot * BLK
            pieces.append(scores[low : low + BLK] + biases[slot])
        scores = jnp.concatenate(pieces, 0)
        top = jnp.max(scores, 0, keepdims=True)
        unscaled = jnp.exp2(scores - top)
        prob = unscaled * (1.0 / jnp.sum(unscaled, 0, keepdims=True))
        row_dot = jnp.sum(prob * dprob, 0, keepdims=True)
        return prob.astype(jnp.bfloat16), (prob * (dprob - row_dot)).astype(jnp.bfloat16)

    gk = jnp.zeros((total, width), jnp.float32)
    gv = jnp.zeros((total, width), jnp.float32)
    ahead = products(slices[0])
    for index, piece in enumerate(slices):
        query, upstream, scores, dprob = ahead
        if index + 1 < len(slices):
            ahead = products(slices[index + 1])
        weights, dscore = softmax(scores, dprob)
        o_out[piece, :] = dot(values_t, weights, (1, 0)).astype(jnp.bfloat16).T
        gq_out[piece, :] = (dot(keys_t, dscore, (1, 0)) * SCALE).astype(jnp.bfloat16).T
        gk = gk + dot(dscore, query, (1, 0))
        gv = gv + dot(weights, upstream, (1, 0))
    at = 0
    for r in range(HEADS_PER_GROUP):
        to = slice(r * width, (r + 1) * width)
        for part in (None, *sends):
            attended, gq = o_out[at : at + rows, :], gq_out[at : at + rows, :]
            if part is None:
                o_own[:, to] = attended
                gq_own[:, to] = gq
            else:
                part[:rows, to] = attended
                part[rows:, to] = gq
            at += rows
    start = (head * (KEY_VALUE_HEADS // head_count) + place[2]) * GROUP_WIDTH
    target = lanes(start, GROUP_WIDTH)
    copies = [
        pltpu.make_async_copy(o_own, o_all.at[:, target], copied.at[0]),
        pltpu.make_async_copy(gq_own, gq_all.at[:, target], copied.at[1]),
    ]
    for copy in copies:
        copy.start()
    gk = (gk * SCALE).astype(jnp.bfloat16)
    gv = gv.astype(jnp.bfloat16)
    for index, grad in enumerate((near_grad, far_grad)):
        here = slice(index * group_rows, (index + 1) * group_rows)
        grad[:group_rows, k_cols] = gk[here]
        grad[:group_rows, v_cols] = gv[here]
        rest = grad.shape[0] - group_rows
        grad[group_rows:, k_cols] = jnp.zeros((rest, width), jnp.bfloat16)
        grad[group_rows:, v_cols] = jnp.zeros((rest, width), jnp.bfloat16)
    for slot in range(slots):
        other, target = placed(slot)
        low = span + slot * BLK
        for index, grad in enumerate((near_grad, far_grad)):

            @pl.when(jnp.logical_and(listed[position, slot] >= 0, other == index))
            def _():
                grad[target, k_cols] = gk[low : low + BLK]
                grad[target, v_cols] = gv[low : low + BLK]

    for copy in copies:
        copy.wait()


def attention(listed, place, own, received, near, far, carried, shape, column):
    head_count, group_rows, store_rows, clean_rows, slots = shape
    rows = own.shape[0] // 2
    total = 2 * group_rows + slots * BLK
    stacked = HEADS_PER_GROUP * group_rows
    smem = pl.BlockSpec(memory_space=pltpu.SMEM)
    vmem = pl.BlockSpec(memory_space=pltpu.VMEM)
    hbm = pl.BlockSpec(memory_space=pl.ANY)
    kept = [i for i, array in enumerate(carried) if not isinstance(array, jax.ShapeDtypeStruct)]
    first_carried = 3 + len(received) + 2
    spaces = [hbm, hbm] + [vmem] * (len(carried) - 2)
    return pl.pallas_call(
        functools.partial(attention_kernel, shape, column, len(kept)),
        in_specs=[smem, smem] + [vmem] * (3 + len(received)) + [spaces[i] for i in kept],
        out_specs=spaces,
        scratch_shapes=[pltpu.VMEM((total, HEAD_SIZE), jnp.bfloat16)] * 2
        + [pltpu.VMEM((stacked, HEAD_SIZE), jnp.bfloat16)] * 4
        + [pltpu.VMEM((rows, GROUP_WIDTH), jnp.bfloat16)] * 2
        + [pltpu.SemaphoreType.DMA((2,))],
        out_shape=[jax.ShapeDtypeStruct(array.shape, jnp.bfloat16) for array in carried],
        input_output_aliases={first_carried + n: i for n, i in enumerate(kept)},
        compiler_params=pltpu.CompilerParams(vmem_limit_bytes=KERNEL_VMEM),
        cost_estimate=pl.CostEstimate(
            flops=8 * group_rows * HEADS_PER_GROUP * HEAD_SIZE * total,
            bytes_accessed=16 * group_rows * GROUP_WIDTH,
            transcendentals=group_rows * HEADS_PER_GROUP * total,
        ),
        name="span_attention",
    )(listed, place, own, *received, near, far, *[carried[i] for i in kept])


def unpack_kernel(head_count, groups, *refs):
    parts, outs = refs[:-4], refs[-4:]
    rows = outs[0].shape[0]
    half = outs[0].shape[1] // head_count
    width = HEAD_SIZE
    for step in range(head_count):
        source = lax.rem(lax.axis_index("head") + step, head_count)
        for group, members in enumerate(groups):
            part = parts[group * head_count + step]
            for at, member in enumerate(members):
                to = lanes(source * half + member * width, width)
                for index in range(2):
                    here = slice((2 * at + index) * width, (2 * at + index + 1) * width)
                    outs[index][:, to] = part[:rows, here]
                    outs[2 + index][:, to] = part[rows:, here]


def unpacked(head_count, groups, grads, rows, clean_rows):
    vmem = pl.BlockSpec(memory_space=pltpu.VMEM)
    parts = [part for chunk in grads for part in chunk]
    width = KEY_VALUE_HEADS * HEAD_SIZE
    return pl.pallas_call(
        functools.partial(unpack_kernel, head_count, groups),
        in_specs=[vmem] * len(parts),
        out_specs=[vmem] * 4,
        out_shape=[jax.ShapeDtypeStruct((rows, width), jnp.bfloat16)] * 2
        + [jax.ShapeDtypeStruct((clean_rows, width), jnp.bfloat16)] * 2,
        name="unpack_gradients",
    )(*parts)


def shards(
    queries,
    noisy_token_keys,
    noisy_token_values,
    clean_token_keys,
    clean_token_values,
    output_gradient,
    history_list,
):
    ctx_count = lax.axis_size("ctx")
    head_count = lax.axis_size("head")
    head = lax.axis_index("head")
    place = jnp.stack([lax.axis_index("ctx"), head]).astype(jnp.int32)
    rows = queries.shape[0]
    clean_rows = clean_token_keys.shape[0]
    store_rows = clean_rows * head_count
    group_rows = rows * head_count
    slots = ctx_count - 2
    per_device = KEY_VALUE_HEADS // head_count
    everything = list(range(per_device))
    half = max(1, per_device // 2)
    key_groups = [g for g in (everything[:half], everything[half:]) if g]
    grad_groups = key_groups
    ask_groups = send_groups = [[m] for m in everything]
    depth = ctx_count // 4
    steps = range(1, head_count)
    row_order = lax.rem(head - jnp.arange(head_count, dtype=jnp.int32) + head_count, head_count)

    def by_block(store):
        if clean_rows >= BLK:
            return store
        return store.reshape(head_count, clean_rows, -1)[row_order].reshape(store.shape)

    packs = packed(
        head_count,
        key_groups,
        noisy_token_keys,
        noisy_token_values,
        clean_token_keys,
        clean_token_values,
    )

    asks = query_blocks(head_count, queries, output_gradient)

    def swap_keys(index):
        return [packs[index][0]] + [shifted(packs[index][step], step) for step in steps]

    def swap_queries(member):
        return [shifted(asks[member][step], step) for step in steps]

    def stored(parts):
        return by_block(jnp.concatenate([part[rows:] for part in parts], 0))

    def along(store):
        return [flipped(store, z << 2) for z in range(1, depth)]

    def joined(parts, line):
        return jnp.concatenate([part[:rows] for part in parts] + [line], 0)

    def summed(near_grad, from_core):
        total = near_grad.astype(jnp.float32) + from_core.astype(jnp.float32)
        return total[:group_rows], total[group_rows:]

    def halved(line):
        middle = line.shape[0] // 2
        return line[:middle], flipped(line[middle:].astype(jnp.bfloat16), 2)

    def back_along(line):
        gives = [line[z * store_rows : (z + 1) * store_rows] for z in range(depth)]
        return gives[0], [
            flipped(give.astype(jnp.bfloat16), z << 2) for z, give in enumerate(gives[1:], 1)
        ]

    def added(keep, others):
        for other in others:
            keep = keep + other.astype(jnp.float32)
        return keep

    together = lax.optimization_barrier
    def swap_heads(noisy_sum, store_sum):
        if clean_rows < BLK:
            store_sum = store_sum.reshape(head_count, clean_rows, -1)[row_order].reshape(
                store_sum.shape
            )
        store_sum = store_sum.astype(jnp.bfloat16)
        noisy_sum = noisy_sum.astype(jnp.bfloat16)
        mixed = [
            jnp.concatenate(
                [
                    noisy_sum[step * rows : (step + 1) * rows],
                    store_sum[step * clean_rows : (step + 1) * clean_rows],
                ],
                0,
            )
            for step in range(head_count)
        ]
        return [mixed[0]] + [shifted(mixed[step], -step) for step in steps]

    shape = (head_count, group_rows, store_rows, clean_rows, slots)
    received = {}
    two = len(key_groups) > 1
    parts = swap_keys(0)
    store = stored(parts)
    others = along(store)
    if two:
        asks[0], parts = together((asks[0], parts))
    received[0] = swap_queries(0)
    line = jnp.concatenate([store, *others], 0)
    crossing = flipped(line, 2)
    if two:
        packs[1], received[0], others = together((packs[1], received[0], others))
        later_parts = swap_keys(1)
        asks[1], later_parts = together((asks[1], later_parts))
        received[1] = swap_queries(1)
        later_store = stored(later_parts)
        later_others = along(later_store)
    near = joined(parts, jnp.concatenate([line, crossing], 0))
    if two:
        near, asks[2], later_parts = together((near, asks[2], later_parts))
        received[2] = swap_queries(2)
    keys = {0: (near, flipped(near, 1))}
    outputs = [jax.ShapeDtypeStruct(queries.shape, jnp.bfloat16)] * 2
    sent = []
    held = []
    waiting = []

    def group_of(groups, member):
        return next(i for i, group in enumerate(groups) if member in group)

    for member in everything:
        k = group_of(key_groups, member)
        first = member == key_groups[k][0]
        last = member == key_groups[k][-1]
        sends = [jax.ShapeDtypeStruct((2 * rows, GROUP_WIDTH), jnp.bfloat16)] * (head_count - 1)
        if first:
            width = len(key_groups[k]) * 2 * HEAD_SIZE
            pair = [jax.ShapeDtypeStruct((near.shape[0], width), jnp.bfloat16)] * 2
        column = key_groups[k].index(member)
        outputs[0], outputs[1], *rest = attention(
            history_list,
            jnp.concatenate([place, jnp.array([member], jnp.int32)]),
            asks[member][0],
            received[member],
            *keys[k],
            [*outputs, *sends, *pair],
            shape,
            column,
        )
        sends, pair = rest[:-2], rest[-2:]
        if two and member == 0:
            outputs, later_others, received[1], received[2] = together(
                (outputs, later_others, received[1], received[2])
            )
            later_line = jnp.concatenate([later_store, *later_others], 0)
            crossing = flipped(later_line, 2)
        if two and member == 1:
            outputs, crossing = together((outputs, crossing))
            near = joined(later_parts, jnp.concatenate([later_line, crossing], 0))
            keys[1] = (near, flipped(near, 1))
        if member + 3 < per_device:
            asks, outputs = together((asks, outputs))
            received[member + 3] = swap_queries(member + 3)
        if two and member == 1:
            pair, received[3] = together((pair, received[3]))
        held.append(sends)
        if two and member == half:
            held[half - 1], outputs = together((held[half - 1], outputs))
        if not two or member >= half - 1:
            later = len(held) if member == everything[-1] else len(held) - 1
            for block_set in held[len(sent) : later]:
                sent.append([shifted(block, -step) for step, block in zip(steps, block_set)])
        if waiting and not last:
            noisy_sum, line = summed(*waiting[0])
            line, outputs, sent[0] = together((line, outputs, sent[0]))
            waiting[0] = (noisy_sum, *halved(line))
        if last:
            if waiting:
                waiting[0], pair, sent[:half] = together((waiting[0], pair, sent[:half]))
            waiting.append((pair[0], flipped(pair[1], 1)))
    grads = []
    if two:
        first_noisy, keep, other = waiting[0]
        keep, others = back_along(added(keep, [other]))
    noisy_sum, line = summed(*waiting[-1])
    last_keep, last_other = halved(line)
    if two:
        last_other, others, sent[:half] = together((last_other, others, sent[:half]))
        grads.append(swap_heads(first_noisy, added(keep, others)))
    last_keep, last_others = back_along(added(last_keep, [last_other]))
    line = added(last_keep, last_others)
    if two:
        line, sent[half:] = together((line, sent[half:]))
    grads.append(swap_heads(noisy_sum, line))
    attended, query_grad = outputs
    for group, blocks in zip(send_groups, sent):
        for step, block in zip(steps, blocks):
            source = lax.rem(head + step, head_count)
            start = (source * per_device + group[0]) * GROUP_WIDTH
            attended = lax.dynamic_update_slice_in_dim(attended, block[:rows], start, 1)
            query_grad = lax.dynamic_update_slice_in_dim(query_grad, block[rows:], start, 1)
    finished = unpacked(head_count, grad_groups, grads, rows, clean_rows)
    return (attended, query_grad, *finished)


def solution(mesh):
    split = P(("ctx", "head"), None)
    return jax.shard_map(
        shards,
        mesh=mesh,
        in_specs=(split, split, split, split, split, split, P()),
        out_specs=(split,) * 6,
        check_vma=False,
    )
```

profile of v0, /device:TPU:0, one launch (start us, length us, event | category | flops | bytes accessed | tf_op | source)
XLA Modules:
  0.0 97.8 jit_solution(58267909202986698)
XLA Ops:
  0.6 2.0 %pack_keys_values.1 = (bf16[128,512]{1,0:T(8,128)(2,1)}, bf16[128,512]{1,0:T(8,128)(2,1)}, bf16[128,512]{1,0:T(8,128)(2,1)}, bf16[128,512]{1,0:T(8,128)(2,1)}) custom-call(bf16[96,1024]{1,0:T(8,128)(2,1)} %k_noisy.1, bf16[96,1024]{1,0:T(8,128)(2,1)} %v_noisy.1, bf16[32,1024]{1,0:T(8,128)(2,1)} %k_clean.1, bf16[32,1024]{1,0:T(8,128)(2,1)} %v_clean.1), custom_call_target="tpu_custom_call" | custom-call | tf_op jit(solution)/shard_map/pack_keys_values/pallas_call | solution.py:68
  2.6 3.0 %collective-permute-start = (bf16[128,512]{1,0:T(8,128)(2,1)}, bf16[128,512]{1,0:T(8,128)(2,1)S(1)}, u32[]{:S(2)}, u32[]{:S(2)}) collective-permute-start(bf16[128,512]{1,0:T(8,128)(2,1)} %get-tuple-element.103), channel_id=1, source_target_pairs={{0,1},{1,0},{2,3},{3,2},{4,5},{5,4},{6,7},{7,6},{8,9},{9,8},{10,11... | collective-permute-start | bytes 393224 | tf_op jit(solution)/shard_map/ppermute | solution.py:31
  5.6 3.2 %stack_queries.1 = (bf16[192,768]{1,0:T(8,128)(2,1)}, bf16[192,768]{1,0:T(8,128)(2,1)}, bf16[192,768]{1,0:T(8,128)(2,1)}, bf16[192,768]{1,0:T(8,128)(2,1)}, bf16...) custom-call(bf16[96,6144]{1,0:T(8,128)(2,1)} %q.1, ...), custom_call_target="tpu_custom_call" | custom-call | tf_op jit(solution)/shard_map/stack_queries/pallas_call | solution.py:93
  9.4 1.9 %collective-permute-start.2 = (bf16[64,512]{1,0:T(8,128)(2,1)S(1)}, bf16[64,512]{1,0:T(8,128)(2,1)S(1)}, u32[]{:S(2)}, u32[]{:S(2)}) collective-permute-start(bf16[64,512]{1,0:T(8,128)(2,1)S(1)} %pad_maximum_fusion.4), channel_id=1, source_target_pairs={{0,8},{2,10},{4,12},{6,14},{8,0},{10,2},{12,4},{14,6},{16,24},{18,... | collective-permute-start | bytes 196616 | tf_op jit(solution)/shard_map/ppermute | solution.py:26
  11.2 2.5 %collective-permute-start.4 = (bf16[64,512]{1,0:T(8,128)(2,1)S(1)}, bf16[64,512]{1,0:T(8,128)(2,1)S(1)}, u32[]{:S(2)}, u32[]{:S(2)}) collective-permute-start(bf16[64,512]{1,0:T(8,128)(2,1)S(1)} %pad_maximum_fusion.4), channel_id=1, source_target_pairs={{0,24},{2,26},{4,28},{6,30},{8,16},{10,18},{12,20},{14,22},{16,8},... | collective-permute-start | bytes 196616 | tf_op jit(solution)/shard_map/ppermute | solution.py:26
  13.8 1.5 %collective-permute-start.1 = (bf16[192,768]{1,0:T(8,128)(2,1)}, bf16[192,768]{1,0:T(8,128)(2,1)S(1)}, u32[]{:S(2)}, u32[]{:S(2)}) collective-permute-start(bf16[192,768]{1,0:T(8,128)(2,1)} %get-tuple-element.105), channel_id=1, source_target_pairs={{0,1},{1,0},{2,3},{3,2},{4,5},{5,4},{6,7},{7,6},{8,9},{9,8},{10,11... | collective-permute-start | bytes 884744 | tf_op jit(solution)/shard_map/ppermute | solution.py:31
  15.4 4.2 %collective-permute-done.3 = bf16[64,512]{1,0:T(8,128)(2,1)S(1)} collective-permute-done((bf16[64,512]{1,0:T(8,128)(2,1)S(1)}, bf16[64,512]{1,0:T(8,128)(2,1)S(1)}, u32[]{:S(2)}, u32[]{:S(2)}) %collective-permute-start.3) | collective-permute-done | bytes 65568 | tf_op jit(solution)/shard_map/ppermute | solution.py:26
  19.6 1.6 %collective-permute-start.6 = (bf16[256,512]{1,0:T(8,128)(2,1)S(1)}, bf16[256,512]{1,0:T(8,128)(2,1)S(1)}, u32[]{:S(2)}, u32[]{:S(2)}) collective-permute-start(bf16[256,512]{1,0:T(8,128)(2,1)S(1)} %get-tuple-element.242), channel_id=1, source_target_pairs={{0,4},{2,6},{4,0},{6,2},{8,12},{10,14},{12,8},{14,10},{16,20},{18,... | collective-permute-start | bytes 786440 | tf_op jit(solution)/shard_map/ppermute | solution.py:26
  21.4 1.5 %collective-permute-start.5 = (bf16[128,512]{1,0:T(8,128)(2,1)S(1)}, bf16[128,512]{1,0:T(8,128)(2,1)S(1)}, u32[]{:S(2)}, u32[]{:S(2)}) collective-permute-start(bf16[128,512]{1,0:T(8,128)(2,1)S(1)} %copy-done.17), channel_id=1, source_target_pairs={{0,1},{1,0},{2,3},{3,2},{4,5},{5,4},{6,7},{7,6},{8,9},{9,8},{10,11... | collective-permute-start | bytes 393224 | tf_op jit(solution)/shard_map/ppermute | solution.py:31
  23.0 3.4 %collective-permute-done.6 = bf16[256,512]{1,0:T(8,128)(2,1)S(1)} collective-permute-done((bf16[256,512]{1,0:T(8,128)(2,1)S(1)}, bf16[256,512]{1,0:T(8,128)(2,1)S(1)}, u32[]{:S(2)}, u32[]{:S(2)}) %collective-permute-start.6) | collective-permute-done | bytes 262176 | tf_op jit(solution)/shard_map/ppermute | solution.py:26
  26.4 1.6 %collective-permute-start.12 = (bf16[192,768]{1,0:T(8,128)(2,1)S(1)}, bf16[192,768]{1,0:T(8,128)(2,1)S(1)}, u32[]{:S(2)}, u32[]{:S(2)}) collective-permute-start(bf16[192,768]{1,0:T(8,128)(2,1)S(1)} %copy-done.16), channel_id=1, source_target_pairs={{0,1},{1,0},{2,3},{3,2},{4,5},{5,4},{6,7},{7,6},{8,9},{9,8},{10,11... | collective-permute-start | bytes 884744 | tf_op jit(solution)/shard_map/ppermute | solution.py:31
  28.6 2.6 %collective-permute-start.10 = (bf16[64,512]{1,0:T(8,128)(2,1)S(1)}, bf16[64,512]{1,0:T(8,128)(2,1)S(1)}, u32[]{:S(2)}, u32[]{:S(2)}) collective-permute-start(bf16[64,512]{1,0:T(8,128)(2,1)S(1)} %pad_maximum_fusion.5), channel_id=1, source_target_pairs={{0,24},{2,26},{4,28},{6,30},{8,16},{10,18},{12,20},{14,22},{16,8},... | collective-permute-start | bytes 196616 | tf_op jit(solution)/shard_map/ppermute | solution.py:26
  31.2 1.5 %collective-permute-start.9 = (bf16[64,512]{1,0:T(8,128)(2,1)S(1)}, bf16[64,512]{1,0:T(8,128)(2,1)S(1)}, u32[]{:S(2)}, u32[]{:S(2)}) collective-permute-start(bf16[64,512]{1,0:T(8,128)(2,1)S(1)} %pad_maximum_fusion.5), channel_id=1, source_target_pairs={{0,16},{2,18},{4,20},{6,22},{8,24},{10,26},{12,28},{14,30},{16,0},... | collective-permute-start | bytes 196616 | tf_op jit(solution)/shard_map/ppermute | solution.py:26
  33.4 5.4 %span_attention.4 = (bf16[96,6144]{1,0:T(8,128)(2,1)}, bf16[96,6144]{1,0:T(8,128)(2,1)}, bf16[192,768]{1,0:T(8,128)(2,1)S(1)}, bf16[704,512]{1,0:T(8,128)(2,1)S(1)}, bf16[704,512]{1,0:T(8,128)(2,1)S(1)}) custom-call(s32[16,16]{1,0:T(8,128)S(1)} %copy-done.3, s32[3]{0:T(128)S(1)} %get-tuple-element.249.place, bf16[192,768]{1,0:T(8,128)(2,1)S(1)} %copy-done.4, ...), custom_call_target="tpu_custom_call" | custom-call | flops 981467136 | bytes 2359296 | tf_op jit(solution)/shard_map/span_attention/pallas_call | solution.py:243
  39.3 1.6 %collective-permute-start.14 = (bf16[256,512]{1,0:T(8,128)(2,1)S(1)}, bf16[256,512]{1,0:T(8,128)(2,1)S(1)}, u32[]{:S(2)}, u32[]{:S(2)}) collective-permute-start(bf16[256,512]{1,0:T(8,128)(2,1)S(1)} %get-tuple-element.236), channel_id=1, source_target_pairs={{0,4},{2,6},{4,0},{6,2},{8,12},{10,14},{12,8},{14,10},{16,20},{18,... | collective-permute-start | bytes 786440 | tf_op jit(solution)/shard_map/ppermute | solution.py:26
  40.8 1.5 %collective-permute-start.13 = (bf16[192,768]{1,0:T(8,128)(2,1)S(1)}, bf16[192,768]{1,0:T(8,128)(2,1)S(1)}, u32[]{:S(2)}, u32[]{:S(2)}) collective-permute-start(bf16[192,768]{1,0:T(8,128)(2,1)S(1)} %copy-done.14), channel_id=1, source_target_pairs={{0,1},{1,0},{2,3},{3,2},{4,5},{5,4},{6,7},{7,6},{8,9},{9,8},{10,11... | collective-permute-start | bytes 884744 | tf_op jit(solution)/shard_map/ppermute | solution.py:31
  42.3 5.4 %span_attention.5 = (bf16[96,6144]{1,0:T(8,128)(2,1)}, bf16[96,6144]{1,0:T(8,128)(2,1)}, bf16[192,768]{1,0:T(8,128)(2,1)S(1)}, bf16[704,512]{1,0:T(8,128)(2,1)S(1)}, bf16[704,512]{1,0:T(8,128)(2,1)S(1)}) custom-call(s32[16,16]{1,0:T(8,128)S(1)} %copy-done.3, ...), custom_call_target="tpu_custom_call", output_to_operand_aliasing={{0}: (6, {}), {1}: (7, {}), {3}: (8, {}), {4}: (9, {})} | custom-call | flops 981467136 | bytes 2359296 | tf_op jit(solution)/shard_map/span_attention/pallas_call | solution.py:243
  47.8 1.7 %collective-permute-done.13.refs_0_ = bf16[192,768]{1,0:T(8,128)(2,1)S(1)} collective-permute-done((bf16[192,768]{1,0:T(8,128)(2,1)S(1)}, bf16[192,768]{1,0:T(8,128)(2,1)S(1)}, u32[]{:S(2)}, u32[]{:S(2)}) %collective-permute-start.13) | collective-permute-done | bytes 294944 | tf_op jit(solution)/shard_map/ppermute | solution.py:31
  49.5 1.5 %collective-permute-start.17 = (bf16[192,768]{1,0:T(8,128)(2,1)S(1)}, bf16[192,768]{1,0:T(8,128)(2,1)S(1)}, u32[]{:S(2)}, u32[]{:S(2)}) collective-permute-start(bf16[192,768]{1,0:T(8,128)(2,1)S(1)} %get-tuple-element.160), channel_id=1, source_target_pairs={{0,1},{1,0},{2,3},{3,2},{4,5},{5,4},{6,7},{7,6},{8,9},{9,8},{10,11... | collective-permute-start | bytes 884744 | tf_op jit(solution)/shard_map/ppermute | solution.py:31
  51.0 5.4 %span_attention.6 = (bf16[96,6144]{1,0:T(8,128)(2,1)}, bf16[96,6144]{1,0:T(8,128)(2,1)}, bf16[192,768]{1,0:T(8,128)(2,1)S(1)}, bf16[704,512]{1,0:T(8,128)(2,1)S(1)}, bf16[704,512]{1,0:T(8,128)(2,1)S(1)}) custom-call(s32[16,16]{1,0:T(8,128)S(1)} %copy-done.3, s32[3]{0:T(128)S(1)} %get-tuple-element.198.place, ...), custom_call_target="tpu_custom_call", output_to_operand_aliasing={{0}: (6, {}), {1}: (7, {})} | custom-call | flops 981467136 | bytes 2359296 | tf_op jit(solution)/shard_map/span_attention/pallas_call | solution.py:243
  57.3 1.6 %collective-permute-done.17 = bf16[192,768]{1,0:T(8,128)(2,1)S(1)} collective-permute-done((bf16[192,768]{1,0:T(8,128)(2,1)S(1)}, bf16[192,768]{1,0:T(8,128)(2,1)S(1)}, u32[]{:S(2)}, u32[]{:S(2)}) %collective-permute-start.17) | collective-permute-done | bytes 294944 | tf_op jit(solution)/shard_map/ppermute | solution.py:31
  59.7 5.4 %span_attention.7 = (bf16[96,6144]{1,0:T(8,128)(2,1)}, bf16[96,6144]{1,0:T(8,128)(2,1)}, bf16[192,768]{1,0:T(8,128)(2,1)S(1)}, bf16[704,512]{1,0:T(8,128)(2,1)S(1)}, bf16[704,512]{1,0:T(8,128)(2,1)S(1)}) custom-call(s32[16,16]{1,0:T(8,128)S(1)} %copy-done.3, ...), custom_call_target="tpu_custom_call", output_to_operand_aliasing={{0}: (6, {}), {1}: (7, {}), {3}: (8, {}), {4}: (9, {})} | custom-call | flops 981467136 | bytes 2359296 | tf_op jit(solution)/shard_map/span_attention/pallas_call | solution.py:243
  65.1 1.9 %collective-permute-done.18 = bf16[256,512]{1,0:T(8,128)(2,1)S(1)} collective-permute-done((bf16[256,512]{1,0:T(8,128)(2,1)S(1)}, bf16[256,512]{1,0:T(8,128)(2,1)S(1)}, u32[]{:S(2)}, u32[]{:S(2)}) %collective-permute-start.18) | collective-permute-done | bytes 262176 | tf_op jit(solution)/shard_map/ppermute | solution.py:26
  67.8 1.5 %collective-permute-start.28 = (bf16[192,768]{1,0:T(8,128)(2,1)S(1)}, bf16[192,768]{1,0:T(8,128)(2,1)S(1)}, u32[]{:S(2)}, u32[]{:S(2)}) collective-permute-start(bf16[192,768]{1,0:T(8,128)(2,1)S(1)} %get-tuple-element.180), channel_id=1, source_target_pairs={{0,1},{1,0},{2,3},{3,2},{4,5},{5,4},{6,7},{7,6},{8,9},{9,8},{10,11... | collective-permute-start | bytes 884744 | tf_op jit(solution)/shard_map/ppermute | solution.py:31
  71.3 2.6 %collective-permute-start.24 = (bf16[64,512]{1,0:T(8,128)(2,1)S(1)}, bf16[64,512]{1,0:T(8,128)(2,1)S(1)}, u32[]{:S(2)}, u32[]{:S(2)}) collective-permute-start(bf16[64,512]{1,0:T(8,128)(2,1)S(1)} %get-tuple-element.215), channel_id=1, source_target_pairs={{0,24},{2,26},{4,28},{6,30},{8,16},{10,18},{12,20},{14,22},{16,8},... | collective-permute-start | bytes 196616 | tf_op jit(solution)/shard_map/ppermute | solution.py:26
  74.0 1.8 %collective-permute-start.22 = (bf16[64,512]{1,0:T(8,128)(2,1)S(1)}, bf16[64,512]{1,0:T(8,128)(2,1)S(1)}, u32[]{:S(2)}, u32[]{:S(2)}) collective-permute-start(bf16[64,512]{1,0:T(8,128)(2,1)S(1)} %get-tuple-element.217), channel_id=1, source_target_pairs={{0,8},{2,10},{4,12},{6,14},{8,0},{10,2},{12,4},{14,6},{16,24},{18,... | collective-permute-start | bytes 196616 | tf_op jit(solution)/shard_map/ppermute | solution.py:26
  75.8 2.2 %collective-permute-done.24 = bf16[64,512]{1,0:T(8,128)(2,1)S(1)} collective-permute-done((bf16[64,512]{1,0:T(8,128)(2,1)S(1)}, bf16[64,512]{1,0:T(8,128)(2,1)S(1)}, u32[]{:S(2)}, u32[]{:S(2)}) %collective-permute-start.24) | collective-permute-done | bytes 65568 | tf_op jit(solution)/shard_map/ppermute | solution.py:26
  81.0 1.9 %collective-permute-start.27 = (bf16[64,512]{1,0:T(8,128)(2,1)S(1)}, bf16[64,512]{1,0:T(8,128)(2,1)S(1)}, u32[]{:S(2)}, u32[]{:S(2)}) collective-permute-start(bf16[64,512]{1,0:T(8,128)(2,1)S(1)} %get-tuple-element.213), channel_id=1, source_target_pairs={{0,24},{2,26},{4,28},{6,30},{8,16},{10,18},{12,20},{14,22},{16,8},... | collective-permute-start | bytes 196616 | tf_op jit(solution)/shard_map/ppermute | solution.py:26
  86.4 1.3 %collective-permute-done.27 = bf16[64,512]{1,0:T(8,128)(2,1)S(1)} collective-permute-done((bf16[64,512]{1,0:T(8,128)(2,1)S(1)}, bf16[64,512]{1,0:T(8,128)(2,1)S(1)}, u32[]{:S(2)}, u32[]{:S(2)}) %collective-permute-start.27) | collective-permute-done | bytes 65568 | tf_op jit(solution)/shard_map/ppermute | solution.py:26
  87.7 2.2 %collective-permute-done.26 = bf16[64,512]{1,0:T(8,128)(2,1)S(1)} collective-permute-done((bf16[64,512]{1,0:T(8,128)(2,1)S(1)}, bf16[64,512]{1,0:T(8,128)(2,1)S(1)}, u32[]{:S(2)}, u32[]{:S(2)}) %collective-permute-start.26) | collective-permute-done | bytes 65568 | tf_op jit(solution)/shard_map/ppermute | solution.py:26
  93.3 1.9 %collective-permute-done.31.refs_3_ = bf16[128,512]{1,0:T(8,128)(2,1)S(1)} collective-permute-done((bf16[128,512]{1,0:T(8,128)(2,1)S(1)}, bf16[128,512]{1,0:T(8,128)(2,1)S(1)}, u32[]{:S(2)}, u32[]{:S(2)}) %collective-permute-start.31) | collective-permute-done | bytes 131104 | tf_op jit(solution)/shard_map/ppermute | solution.py:31
  95.9 2.0 %unpack_gradients.1 = (bf16[96,1024]{1,0:T(8,128)(2,1)}, bf16[96,1024]{1,0:T(8,128)(2,1)}, bf16[32,1024]{1,0:T(8,128)(2,1)}, bf16[32,1024]{1,0:T(8,128)(2,1)}) custom-call(bf16[128,512]{1,0:T(8,128)(2,1)} %get-tuple-element.251.refs_0_, bf16[128,512]{1,0:T(8,128)(2,1)} %copy-done.12, bf16[128,512]{1,0:T(8,128)(2,1)} %get-tuple-element.252.refs_2_, ...), custom_call_target="tpu_custom_call" | custom-call | tf_op jit(solution)/shard_map/unpack_gradients/pallas_call | solution.py:284
  (119 shorter events, 17.7 us)
Async XLA Ops:
  2.6 6.7 %collective-permute-start = (bf16[128,512]{1,0:T(8,128)(2,1)}, bf16[128,512]{1,0:T(8,128)(2,1)S(1)}, u32[]{:S(2)}, u32[]{:S(2)}) collective-permute-start(bf16[128,512]{1,0:T(8,128)(2,1)} %get-tuple-element.103), channel_id=1, source_target_pairs={{0,1},{1,0},{2,3},{3,2},{4,5},{5,4},{6,7},{7,6},{8,9},{9,8},{10,11... | collective-permute-start | bytes 393224 | tf_op jit(solution)/shard_map/ppermute | solution.py:31
  9.4 6.0 %collective-permute-start.2 = (bf16[64,512]{1,0:T(8,128)(2,1)S(1)}, bf16[64,512]{1,0:T(8,128)(2,1)S(1)}, u32[]{:S(2)}, u32[]{:S(2)}) collective-permute-start(bf16[64,512]{1,0:T(8,128)(2,1)S(1)} %pad_maximum_fusion.4), channel_id=1, source_target_pairs={{0,8},{2,10},{4,12},{6,14},{8,0},{10,2},{12,4},{14,6},{16,24},{18,... | collective-permute-start | bytes 196616 | tf_op jit(solution)/shard_map/ppermute | solution.py:26
  11.2 8.4 %collective-permute-start.4 = (bf16[64,512]{1,0:T(8,128)(2,1)S(1)}, bf16[64,512]{1,0:T(8,128)(2,1)S(1)}, u32[]{:S(2)}, u32[]{:S(2)}) collective-permute-start(bf16[64,512]{1,0:T(8,128)(2,1)S(1)} %pad_maximum_fusion.4), channel_id=1, source_target_pairs={{0,24},{2,26},{4,28},{6,30},{8,16},{10,18},{12,20},{14,22},{16,8},... | collective-permute-start | bytes 196616 | tf_op jit(solution)/shard_map/ppermute | solution.py:26
  13.7 5.9 %collective-permute-start.3 = (bf16[64,512]{1,0:T(8,128)(2,1)S(1)}, bf16[64,512]{1,0:T(8,128)(2,1)S(1)}, u32[]{:S(2)}, u32[]{:S(2)}) collective-permute-start(bf16[64,512]{1,0:T(8,128)(2,1)S(1)} %pad_maximum_fusion.4), channel_id=1, source_target_pairs={{0,16},{2,18},{4,20},{6,22},{8,24},{10,26},{12,28},{14,30},{16,0},... | collective-permute-start | bytes 196616 | tf_op jit(solution)/shard_map/ppermute | solution.py:26
  13.8 7.5 %collective-permute-start.1 = (bf16[192,768]{1,0:T(8,128)(2,1)}, bf16[192,768]{1,0:T(8,128)(2,1)S(1)}, u32[]{:S(2)}, u32[]{:S(2)}) collective-permute-start(bf16[192,768]{1,0:T(8,128)(2,1)} %get-tuple-element.105), channel_id=1, source_target_pairs={{0,1},{1,0},{2,3},{3,2},{4,5},{5,4},{6,7},{7,6},{8,9},{9,8},{10,11... | collective-permute-start | bytes 884744 | tf_op jit(solution)/shard_map/ppermute | solution.py:31
  19.6 6.7 %collective-permute-start.6 = (bf16[256,512]{1,0:T(8,128)(2,1)S(1)}, bf16[256,512]{1,0:T(8,128)(2,1)S(1)}, u32[]{:S(2)}, u32[]{:S(2)}) collective-permute-start(bf16[256,512]{1,0:T(8,128)(2,1)S(1)} %get-tuple-element.242), channel_id=1, source_target_pairs={{0,4},{2,6},{4,0},{6,2},{8,12},{10,14},{12,8},{14,10},{16,20},{18,... | collective-permute-start | bytes 786440 | tf_op jit(solution)/shard_map/ppermute | solution.py:26
  21.4 5.0 %collective-permute-start.5 = (bf16[128,512]{1,0:T(8,128)(2,1)S(1)}, bf16[128,512]{1,0:T(8,128)(2,1)S(1)}, u32[]{:S(2)}, u32[]{:S(2)}) collective-permute-start(bf16[128,512]{1,0:T(8,128)(2,1)S(1)} %copy-done.17), channel_id=1, source_target_pairs={{0,1},{1,0},{2,3},{3,2},{4,5},{5,4},{6,7},{7,6},{8,9},{9,8},{10,11... | collective-permute-start | bytes 393224 | tf_op jit(solution)/shard_map/ppermute | solution.py:31
  26.4 12.8 %collective-permute-start.12 = (bf16[192,768]{1,0:T(8,128)(2,1)S(1)}, bf16[192,768]{1,0:T(8,128)(2,1)S(1)}, u32[]{:S(2)}, u32[]{:S(2)}) collective-permute-start(bf16[192,768]{1,0:T(8,128)(2,1)S(1)} %copy-done.16), channel_id=1, source_target_pairs={{0,1},{1,0},{2,3},{3,2},{4,5},{5,4},{6,7},{7,6},{8,9},{9,8},{10,11... | collective-permute-start | bytes 884744 | tf_op jit(solution)/shard_map/ppermute | solution.py:31
  28.0 11.2 %collective-permute-start.11 = (bf16[192,768]{1,0:T(8,128)(2,1)S(1)}, bf16[192,768]{1,0:T(8,128)(2,1)S(1)}, u32[]{:S(2)}, u32[]{:S(2)}) collective-permute-start(bf16[192,768]{1,0:T(8,128)(2,1)S(1)} %copy-done.15), channel_id=1, source_target_pairs={{0,1},{1,0},{2,3},{3,2},{4,5},{5,4},{6,7},{7,6},{8,9},{9,8},{10,11... | collective-permute-start | bytes 884744 | tf_op jit(solution)/shard_map/ppermute | solution.py:31
  28.5 4.3 %collective-permute-start.7 = (bf16[704,512]{1,0:T(8,128)(2,1)S(1)}, bf16[704,512]{1,0:T(8,128)(2,1)S(1)}, u32[]{:S(2)}, u32[]{:S(2)}) collective-permute-start(bf16[704,512]{1,0:T(8,128)(2,1)S(1)} %constant_dynamic-update-slice_fusion.5.refs_1_), channel_id=1, source_target_pairs={{0,2},{2,0},{4,6},{6,4},{8,10},{10,8},{12,14},{14,12},{16,18},{18,... | collective-permute-start | bytes 2162696 | tf_op jit(solution)/shard_map/ppermute | solution.py:26
  28.6 10.1 %collective-permute-start.10 = (bf16[64,512]{1,0:T(8,128)(2,1)S(1)}, bf16[64,512]{1,0:T(8,128)(2,1)S(1)}, u32[]{:S(2)}, u32[]{:S(2)}) collective-permute-start(bf16[64,512]{1,0:T(8,128)(2,1)S(1)} %pad_maximum_fusion.5), channel_id=1, source_target_pairs={{0,24},{2,26},{4,28},{6,30},{8,16},{10,18},{12,20},{14,22},{16,8},... | collective-permute-start | bytes 196616 | tf_op jit(solution)/shard_map/ppermute | solution.py:26
  31.2 7.9 %collective-permute-start.9 = (bf16[64,512]{1,0:T(8,128)(2,1)S(1)}, bf16[64,512]{1,0:T(8,128)(2,1)S(1)}, u32[]{:S(2)}, u32[]{:S(2)}) collective-permute-start(bf16[64,512]{1,0:T(8,128)(2,1)S(1)} %pad_maximum_fusion.5), channel_id=1, source_target_pairs={{0,16},{2,18},{4,20},{6,22},{8,24},{10,26},{12,28},{14,30},{16,0},... | collective-permute-start | bytes 196616 | tf_op jit(solution)/shard_map/ppermute | solution.py:26
  32.8 6.4 %collective-permute-start.8 = (bf16[64,512]{1,0:T(8,128)(2,1)S(1)}, bf16[64,512]{1,0:T(8,128)(2,1)S(1)}, u32[]{:S(2)}, u32[]{:S(2)}) collective-permute-start(bf16[64,512]{1,0:T(8,128)(2,1)S(1)} %pad_maximum_fusion.5), channel_id=1, source_target_pairs={{0,8},{2,10},{4,12},{6,14},{8,0},{10,2},{12,4},{14,6},{16,24},{18,... | collective-permute-start | bytes 196616 | tf_op jit(solution)/shard_map/ppermute | solution.py:26
  39.3 8.5 %collective-permute-start.14 = (bf16[256,512]{1,0:T(8,128)(2,1)S(1)}, bf16[256,512]{1,0:T(8,128)(2,1)S(1)}, u32[]{:S(2)}, u32[]{:S(2)}) collective-permute-start(bf16[256,512]{1,0:T(8,128)(2,1)S(1)} %get-tuple-element.236), channel_id=1, source_target_pairs={{0,4},{2,6},{4,0},{6,2},{8,12},{10,14},{12,8},{14,10},{16,20},{18,... | collective-permute-start | bytes 786440 | tf_op jit(solution)/shard_map/ppermute | solution.py:26
  40.8 8.7 %collective-permute-start.13 = (bf16[192,768]{1,0:T(8,128)(2,1)S(1)}, bf16[192,768]{1,0:T(8,128)(2,1)S(1)}, u32[]{:S(2)}, u32[]{:S(2)}) collective-permute-start(bf16[192,768]{1,0:T(8,128)(2,1)S(1)} %copy-done.14), channel_id=1, source_target_pairs={{0,1},{1,0},{2,3},{3,2},{4,5},{5,4},{6,7},{7,6},{8,9},{9,8},{10,11... | collective-permute-start | bytes 884744 | tf_op jit(solution)/shard_map/ppermute | solution.py:31
  47.8 3.3 %collective-permute-start.15 = (bf16[704,512]{1,0:T(8,128)(2,1)S(1)}, bf16[704,512]{1,0:T(8,128)(2,1)S(1)}, u32[]{:S(2)}, u32[]{:S(2)}) collective-permute-start(bf16[704,512]{1,0:T(8,128)(2,1)S(1)} %constant_dynamic-update-slice_fusion.16.refs_1_), channel_id=1, source_target_pairs={{0,2},{2,0},{4,6},{6,4},{8,10},{10,8},{12,14},{14,12},{16,18},{18,... | collective-permute-start | bytes 2162696 | tf_op jit(solution)/shard_map/ppermute | solution.py:26
  49.5 7.5 %collective-permute-start.16 = (bf16[704,512]{1,0:T(8,128)(2,1)S(1)}, bf16[704,512]{1,0:T(8,128)(2,1)S(1)}, u32[]{:S(2)}, u32[]{:S(2)}) collective-permute-start(bf16[704,512]{1,0:T(8,128)(2,1)S(1)} %get-tuple-element.150), channel_id=1, source_target_pairs={{0,2},{2,0},{4,6},{6,4},{8,10},{10,8},{12,14},{14,12},{16,18},{18,... | collective-permute-start | bytes 2162696 | tf_op jit(solution)/shard_map/ppermute | solution.py:26
  49.5 9.4 %collective-permute-start.17 = (bf16[192,768]{1,0:T(8,128)(2,1)S(1)}, bf16[192,768]{1,0:T(8,128)(2,1)S(1)}, u32[]{:S(2)}, u32[]{:S(2)}) collective-permute-start(bf16[192,768]{1,0:T(8,128)(2,1)S(1)} %get-tuple-element.160), channel_id=1, source_target_pairs={{0,1},{1,0},{2,3},{3,2},{4,5},{5,4},{6,7},{7,6},{8,9},{9,8},{10,11... | collective-permute-start | bytes 884744 | tf_op jit(solution)/shard_map/ppermute | solution.py:31
  56.4 10.6 %collective-permute-start.19 = (bf16[192,768]{1,0:T(8,128)(2,1)S(1)}, bf16[192,768]{1,0:T(8,128)(2,1)S(1)}, u32[]{:S(2)}, u32[]{:S(2)}) collective-permute-start(bf16[192,768]{1,0:T(8,128)(2,1)S(1)} %get-tuple-element.170), channel_id=1, source_target_pairs={{0,1},{1,0},{2,3},{3,2},{4,5},{5,4},{6,7},{7,6},{8,9},{9,8},{10,11... | collective-permute-start | bytes 884744 | tf_op jit(solution)/shard_map/ppermute | solution.py:31
  59.0 8.0 %collective-permute-start.18 = (bf16[256,512]{1,0:T(8,128)(2,1)S(1)}, bf16[256,512]{1,0:T(8,128)(2,1)S(1)}, u32[]{:S(2)}, u32[]{:S(2)}) collective-permute-start(bf16[256,512]{1,0:T(8,128)(2,1)S(1)} %slice.223), channel_id=1, source_target_pairs={{0,4},{2,6},{4,0},{6,2},{8,12},{10,14},{12,8},{14,10},{16,20},{18,... | collective-permute-start | bytes 786440 | tf_op jit(solution)/shard_map/ppermute | solution.py:26
  67.8 2.6 %collective-permute-start.20 = (bf16[704,512]{1,0:T(8,128)(2,1)S(1)}, bf16[704,512]{1,0:T(8,128)(2,1)S(1)}, u32[]{:S(2)}, u32[]{:S(2)}) collective-permute-start(bf16[704,512]{1,0:T(8,128)(2,1)S(1)} %get-tuple-element.172), channel_id=1, source_target_pairs={{0,2},{2,0},{4,6},{6,4},{8,10},{10,8},{12,14},{14,12},{16,18},{18,... | collective-permute-start | bytes 2162696 | tf_op jit(solution)/shard_map/ppermute | solution.py:26
  67.8 22.1 %collective-permute-start.28 = (bf16[192,768]{1,0:T(8,128)(2,1)S(1)}, bf16[192,768]{1,0:T(8,128)(2,1)S(1)}, u32[]{:S(2)}, u32[]{:S(2)}) collective-permute-start(bf16[192,768]{1,0:T(8,128)(2,1)S(1)} %get-tuple-element.180), channel_id=1, source_target_pairs={{0,1},{1,0},{2,3},{3,2},{4,5},{5,4},{6,7},{7,6},{8,9},{9,8},{10,11... | collective-permute-start | bytes 884744 | tf_op jit(solution)/shard_map/ppermute | solution.py:31
  70.7 9.2 %collective-permute-start.21 = (bf16[256,512]{1,0:T(8,128)(2,1)S(1)}, bf16[256,512]{1,0:T(8,128)(2,1)S(1)}, u32[]{:S(2)}, u32[]{:S(2)}) collective-permute-start(bf16[256,512]{1,0:T(8,128)(2,1)S(1)} %slice.171), channel_id=1, source_target_pairs={{0,4},{2,6},{4,0},{6,2},{8,12},{10,14},{12,8},{14,10},{16,20},{18,... | collective-permute-start | bytes 786440 | tf_op jit(solution)/shard_map/ppermute | solution.py:26
  71.3 6.6 %collective-permute-start.24 = (bf16[64,512]{1,0:T(8,128)(2,1)S(1)}, bf16[64,512]{1,0:T(8,128)(2,1)S(1)}, u32[]{:S(2)}, u32[]{:S(2)}) collective-permute-start(bf16[64,512]{1,0:T(8,128)(2,1)S(1)} %get-tuple-element.215), channel_id=1, source_target_pairs={{0,24},{2,26},{4,28},{6,30},{8,16},{10,18},{12,20},{14,22},{16,8},... | collective-permute-start | bytes 196616 | tf_op jit(solution)/shard_map/ppermute | solution.py:26
  73.9 6.0 %collective-permute-start.23 = (bf16[64,512]{1,0:T(8,128)(2,1)S(1)}, bf16[64,512]{1,0:T(8,128)(2,1)S(1)}, u32[]{:S(2)}, u32[]{:S(2)}) collective-permute-start(bf16[64,512]{1,0:T(8,128)(2,1)S(1)} %get-tuple-element.216), channel_id=1, source_target_pairs={{0,16},{2,18},{4,20},{6,22},{8,24},{10,26},{12,28},{14,30},{16,0},... | collective-permute-start | bytes 196616 | tf_op jit(solution)/shard_map/ppermute | solution.py:26
  74.0 6.0 %collective-permute-start.22 = (bf16[64,512]{1,0:T(8,128)(2,1)S(1)}, bf16[64,512]{1,0:T(8,128)(2,1)S(1)}, u32[]{:S(2)}, u32[]{:S(2)}) collective-permute-start(bf16[64,512]{1,0:T(8,128)(2,1)S(1)} %get-tuple-element.217), channel_id=1, source_target_pairs={{0,8},{2,10},{4,12},{6,14},{8,0},{10,2},{12,4},{14,6},{16,24},{18,... | collective-permute-start | bytes 196616 | tf_op jit(solution)/shard_map/ppermute | solution.py:26
  78.0 12.0 %collective-permute-start.29 = (bf16[192,768]{1,0:T(8,128)(2,1)S(1)}, bf16[192,768]{1,0:T(8,128)(2,1)S(1)}, u32[]{:S(2)}, u32[]{:S(2)}) collective-permute-start(bf16[192,768]{1,0:T(8,128)(2,1)S(1)} %get-tuple-element.181), channel_id=1, source_target_pairs={{0,1},{1,0},{2,3},{3,2},{4,5},{5,4},{6,7},{7,6},{8,9},{9,8},{10,11... | collective-permute-start | bytes 884744 | tf_op jit(solution)/shard_map/ppermute | solution.py:31
  80.1 5.0 %collective-permute-start.25 = (bf16[64,512]{1,0:T(8,128)(2,1)S(1)}, bf16[64,512]{1,0:T(8,128)(2,1)S(1)}, u32[]{:S(2)}, u32[]{:S(2)}) collective-permute-start(bf16[64,512]{1,0:T(8,128)(2,1)S(1)} %get-tuple-element.212), channel_id=1, source_target_pairs={{0,8},{2,10},{4,12},{6,14},{8,0},{10,2},{12,4},{14,6},{16,24},{18,... | collective-permute-start | bytes 196616 | tf_op jit(solution)/shard_map/ppermute | solution.py:26
  81.0 6.7 %collective-permute-start.27 = (bf16[64,512]{1,0:T(8,128)(2,1)S(1)}, bf16[64,512]{1,0:T(8,128)(2,1)S(1)}, u32[]{:S(2)}, u32[]{:S(2)}) collective-permute-start(bf16[64,512]{1,0:T(8,128)(2,1)S(1)} %get-tuple-element.213), channel_id=1, source_target_pairs={{0,24},{2,26},{4,28},{6,30},{8,16},{10,18},{12,20},{14,22},{16,8},... | collective-permute-start | bytes 196616 | tf_op jit(solution)/shard_map/ppermute | solution.py:26
  82.9 7.0 %collective-permute-start.26 = (bf16[64,512]{1,0:T(8,128)(2,1)S(1)}, bf16[64,512]{1,0:T(8,128)(2,1)S(1)}, u32[]{:S(2)}, u32[]{:S(2)}) collective-permute-start(bf16[64,512]{1,0:T(8,128)(2,1)S(1)} %get-tuple-element.214), channel_id=1, source_target_pairs={{0,16},{2,18},{4,20},{6,22},{8,24},{10,26},{12,28},{14,30},{16,0},... | collective-permute-start | bytes 196616 | tf_op jit(solution)/shard_map/ppermute | solution.py:26
  85.2 8.1 %collective-permute-start.30 = (bf16[128,512]{1,0:T(8,128)(2,1)S(1)}, bf16[128,512]{1,0:T(8,128)(2,1)S(1)}, u32[]{:S(2)}, u32[]{:S(2)}) collective-permute-start(bf16[128,512]{1,0:T(8,128)(2,1)S(1)} %pad_maximum_fusion.1), channel_id=1, source_target_pairs={{0,1},{1,0},{2,3},{3,2},{4,5},{5,4},{6,7},{7,6},{8,9},{9,8},{10,11... | collective-permute-start | bytes 393224 | tf_op jit(solution)/shard_map/ppermute | solution.py:31
  90.0 5.2 %collective-permute-start.31 = (bf16[128,512]{1,0:T(8,128)(2,1)S(1)}, bf16[128,512]{1,0:T(8,128)(2,1)S(1)}, u32[]{:S(2)}, u32[]{:S(2)}) collective-permute-start(bf16[128,512]{1,0:T(8,128)(2,1)S(1)} %pad_maximum_fusion.3), channel_id=1, source_target_pairs={{0,1},{1,0},{2,3},{3,2},{4,5},{5,4},{6,7},{7,6},{8,9},{9,8},{10,11... | collective-permute-start | bytes 393224 | tf_op jit(solution)/shard_map/ppermute | solution.py:31
  (18 other events, 169.9 us)
where the time goes:
time: 98.1 us; the launch traced here: 97.8 us
  starting transfers between devices  38.3 us (39%)
  Pallas kernels  28.6 us (29%)
  waiting for transfers between devices  22.4 us (23%)
  local copies, waits for them, and re-layouts  4.9 us (5%)
  other arithmetic  2.56 us (3%)
  between operations  1.1 us (1%)
    ppermute x20, starting transfers between devices, flipped(): return lax.ppermute(block, 'ctx', [(i, i ^ bits) for i in range(count)])  21.7 us
    pallas_call x4, Pallas kernels, attention(): pl.pallas_call(functools.partial(attention_kernel, shape, column, len(kep...  21.5 us
    ppermute x12, starting transfers between devices, shifted(): lax.ppermute(block, 'head', [(i, (i + step) % count) for i in range(count)])  16.6 us
    ppermute x20, waiting for transfers between devices, flipped(): return lax.ppermute(block, 'ctx', [(i, i ^ bits) for i in range(count)])  16.6 us
    ppermute x12, waiting for transfers between devices, shifted(): lax.ppermute(block, 'head', [(i, (i + step) % count) for i in range(count)])  5.85 us
    pallas_call x1, Pallas kernels, query_blocks(): pl.pallas_call(functools.partial(stack_kernel, head_count), in_specs=[vme...  3.17 us
    dynamic_update_slice x4, local copies, waits for them, and re-layouts, shards(): lax.dynamic_update_slice_in_dim(query_grad, block[rows:], start, 1)  2.91 us
    pallas_call x1, Pallas kernels, packed(): pl.pallas_call(functools.partial(pack_kernel, head_count, groups), in_spe...  1.97 us
  transfers between devices with their start and end apart: 32, of which 13 were waited for; matrix products, arithmetic and copies ran while one was open for 6% of the time, Pallas kernels for 25%

commit v1 on v0

--- a/solution.py
+++ b/solution.py
@@ -350,13 +350,17 @@
     def joined(parts, line):
         return jnp.concatenate([part[:rows] for part in parts] + [line], 0)
 
-    def summed(near_grad, from_core):
-        total = near_grad.astype(jnp.float32) + from_core.astype(jnp.float32)
-        return total[:group_rows], total[group_rows:]
-
-    def halved(line):
-        middle = line.shape[0] // 2
-        return line[:middle], flipped(line[middle:].astype(jnp.bfloat16), 2)
+    def summed(pair, low, high):
+        return pair[0][low:high].astype(jnp.float32) + pair[1][low:high].astype(jnp.float32)
+
+    middle = group_rows + depth * store_rows
+    end = middle + depth * store_rows
+
+    def to_cross(pair):
+        return summed(pair, middle, end).astype(jnp.bfloat16)
+
+    def line_of(pair, other):
+        return summed(pair, group_rows, middle) + other.astype(jnp.float32)
 
     def back_along(line):
         gives = [line[z * store_rows : (z + 1) * store_rows] for z in range(depth)]
@@ -415,7 +419,7 @@
     outputs = [jax.ShapeDtypeStruct(queries.shape, jnp.bfloat16)] * 2
     sent = []
     held = []
-    waiting = []
+    returned = None
 
     def group_of(groups, member):
         return next(i for i, group in enumerate(groups) if member in group)
@@ -462,28 +466,28 @@
             later = len(held) if member == everything[-1] else len(held) - 1
             for block_set in held[len(sent) : later]:
                 sent.append([shifted(block, -step) for step, block in zip(steps, block_set)])
-        if waiting and not last:
-            noisy_sum, line = summed(*waiting[0])
-            line, outputs, sent[0] = together((line, outputs, sent[0]))
-            waiting[0] = (noisy_sum, *halved(line))
-        if last:
-            if waiting:
-                waiting[0], pair, sent[:half] = together((waiting[0], pair, sent[:half]))
-            waiting.append((pair[0], flipped(pair[1], 1)))
+        if two and member == half and not last:
+            first_other, outputs, sent[0] = together((first_other, outputs, sent[0]))
+            returned = back_along(line_of(first_pair, first_other))
+        if last and member == everything[-1]:
+            if two:
+                if returned is None:
+                    returned = back_along(line_of(first_pair, first_other))
+                returned, pair, sent[half - 1] = together((returned, pair, sent[half - 1]))
+            last_pair = (pair[0], flipped(pair[1], 1))
+        elif last:
+            first_pair = (pair[0], flipped(pair[1], 1))
+            first_pair, outputs = together((first_pair, outputs))
+            first_other = flipped(to_cross(first_pair), 2)
     grads = []
     if two:
-        first_noisy, keep, other = waiting[0]
-        keep, others = back_along(added(keep, [other]))
-    noisy_sum, line = summed(*waiting[-1])
-    last_keep, last_other = halved(line)
-    if two:
-        last_other, others, sent[:half] = together((last_other, others, sent[:half]))
-        grads.append(swap_heads(first_noisy, added(keep, others)))
-    last_keep, last_others = back_along(added(last_keep, [last_other]))
-    line = added(last_keep, last_others)
+        sent[:half], _ = together((sent[:half], last_pair))
+        grads.append(swap_heads(summed(first_pair, 0, group_rows), added(*returned)))
+    keep, others = back_along(line_of(last_pair, flipped(to_cross(last_pair), 2)))
+    line = added(keep, others)
     if two:
         line, sent[half:] = together((line, sent[half:]))
-    grads.append(swap_heads(noisy_sum, line))
+    grads.append(swap_heads(summed(last_pair, 0, group_rows), line))
     attended, query_grad = outputs
     for group, blocks in zip(send_groups, sent):
         for step, block in zip(steps, blocks):

time: 98.1 us -> 101 us (1.030)
  other arithmetic: 2.56 us -> 4.31 us
  starting transfers between devices: 38.3 us -> 39.9 us
  waiting for transfers between devices: 22.4 us -> 20.8 us
  local copies, waits for them, and re-layouts: 4.9 us -> 6.03 us
    ppermute x12, waiting for transfers between devices: 5.85 us -> 1.9 us  [shifted(): lax.ppermute(block, 'head', [(i, (i + step) % count) for i in range(count)])]
    ppermute x20, waiting for transfers between devices: 16.6 us -> 18.9 us  [flipped(): return lax.ppermute(block, 'ctx', [(i, i ^ bits) for i in range(count)])]
    convert_element_type x0 -> x4, other arithmetic: none -> 2.11 us  [the longest x2 1.08 us: to_cross(): return summed(pair, middle, end).astype(jnp.bfloat16)]
    unnamed x48 -> x44, local copies, waits for them, and re-layouts: 1.67 us -> 2.97 us
  transfers between devices with their start and end apart: 32 -> 32, of which waited for: 13 -> 12; matrix products, arithmetic and copies ran while one was open for 6% -> 7% of each run, Pallas kernels for 25% -> 24%
where the time goes in v1:
time: 101 us
  starting transfers between devices  39.9 us (40%)
  Pallas kernels  28.5 us (28%)
  waiting for transfers between devices  20.8 us (21%)
  local copies, waits for them, and re-layouts  6.03 us (6%)
  other arithmetic  4.31 us (4%)
  between operations  1.13 us (1%)
    ppermute x20, starting transfers between devices, flipped(): return lax.ppermute(block, 'ctx', [(i, i ^ bits) for i in range(count)])  22.4 us
    pallas_call x4, Pallas kernels, attention(): pl.pallas_call(functools.partial(attention_kernel, shape, column, len(kep...  21.4 us
    ppermute x20, waiting for transfers between devices, flipped(): return lax.ppermute(block, 'ctx', [(i, i ^ bits) for i in range(count)])  18.9 us
    ppermute x12, starting transfers between devices, shifted(): lax.ppermute(block, 'head', [(i, (i + step) % count) for i in range(count)])  17.5 us
    pallas_call x1, Pallas kernels, query_blocks(): pl.pallas_call(functools.partial(stack_kernel, head_count), in_specs=[vme...  3.17 us
    unnamed x44, local copies, waits for them, and re-layouts  2.97 us
    dynamic_update_slice x4, local copies, waits for them, and re-layouts, shards(): lax.dynamic_update_slice_in_dim(query_grad, block[rows:], start, 1)  2.91 us
  transfers between devices with their start and end apart: 32, of which 12 were waited for; matrix products, arithmetic and copies ran while one was open for 7% of the time, Pallas kernels for 24%

profile of v1, /device:TPU:0, one launch (start us, length us, event | category | flops | bytes accessed | tf_op | source)
XLA Modules:
  0.0 100.7 jit_solution(9581559484312290363)
XLA Ops:
  0.6 2.0 %pack_keys_values.1 = (bf16[128,512]{1,0:T(8,128)(2,1)}, bf16[128,512]{1,0:T(8,128)(2,1)}, bf16[128,512]{1,0:T(8,128)(2,1)}, bf16[128,512]{1,0:T(8,128)(2,1)}) custom-call(bf16[96,1024]{1,0:T(8,128)(2,1)} %k_noisy.1, bf16[96,1024]{1,0:T(8,128)(2,1)} %v_noisy.1, bf16[32,1024]{1,0:T(8,128)(2,1)} %k_clean.1, bf16[32,1024]{1,0:T(8,128)(2,1)} %v_clean.1), custom_call_target="tpu_custom_call" | custom-call | tf_op jit(solution)/shard_map/pack_keys_values/pallas_call | solution.py:68
  2.6 3.0 %collective-permute-start = (bf16[128,512]{1,0:T(8,128)(2,1)}, bf16[128,512]{1,0:T(8,128)(2,1)S(1)}, u32[]{:S(2)}, u32[]{:S(2)}) collective-permute-start(bf16[128,512]{1,0:T(8,128)(2,1)} %get-tuple-element.103), channel_id=1, source_target_pairs={{0,1},{1,0},{2,3},{3,2},{4,5},{5,4},{6,7},{7,6},{8,9},{9,8},{10,11... | collective-permute-start | bytes 393224 | tf_op jit(solution)/shard_map/ppermute | solution.py:31
  5.6 3.2 %stack_queries.1 = (bf16[192,768]{1,0:T(8,128)(2,1)}, bf16[192,768]{1,0:T(8,128)(2,1)}, bf16[192,768]{1,0:T(8,128)(2,1)}, bf16[192,768]{1,0:T(8,128)(2,1)}, bf16...) custom-call(bf16[96,6144]{1,0:T(8,128)(2,1)} %q.1, ...), custom_call_target="tpu_custom_call" | custom-call | tf_op jit(solution)/shard_map/stack_queries/pallas_call | solution.py:93
  9.4 1.9 %collective-permute-start.2 = (bf16[64,512]{1,0:T(8,128)(2,1)S(1)}, bf16[64,512]{1,0:T(8,128)(2,1)S(1)}, u32[]{:S(2)}, u32[]{:S(2)}) collective-permute-start(bf16[64,512]{1,0:T(8,128)(2,1)S(1)} %pad_maximum_fusion.4), channel_id=1, source_target_pairs={{0,8},{2,10},{4,12},{6,14},{8,0},{10,2},{12,4},{14,6},{16,24},{18,... | collective-permute-start | bytes 196616 | tf_op jit(solution)/shard_map/ppermute | solution.py:26
  11.2 2.5 %collective-permute-start.4 = (bf16[64,512]{1,0:T(8,128)(2,1)S(1)}, bf16[64,512]{1,0:T(8,128)(2,1)S(1)}, u32[]{:S(2)}, u32[]{:S(2)}) collective-permute-start(bf16[64,512]{1,0:T(8,128)(2,1)S(1)} %pad_maximum_fusion.4), channel_id=1, source_target_pairs={{0,24},{2,26},{4,28},{6,30},{8,16},{10,18},{12,20},{14,22},{16,8},... | collective-permute-start | bytes 196616 | tf_op jit(solution)/shard_map/ppermute | solution.py:26
  13.8 1.5 %collective-permute-start.1 = (bf16[192,768]{1,0:T(8,128)(2,1)}, bf16[192,768]{1,0:T(8,128)(2,1)S(1)}, u32[]{:S(2)}, u32[]{:S(2)}) collective-permute-start(bf16[192,768]{1,0:T(8,128)(2,1)} %get-tuple-element.105), channel_id=1, source_target_pairs={{0,1},{1,0},{2,3},{3,2},{4,5},{5,4},{6,7},{7,6},{8,9},{9,8},{10,11... | collective-permute-start | bytes 884744 | tf_op jit(solution)/shard_map/ppermute | solution.py:31
  15.4 4.2 %collective-permute-done.3 = bf16[64,512]{1,0:T(8,128)(2,1)S(1)} collective-permute-done((bf16[64,512]{1,0:T(8,128)(2,1)S(1)}, bf16[64,512]{1,0:T(8,128)(2,1)S(1)}, u32[]{:S(2)}, u32[]{:S(2)}) %collective-permute-start.3) | collective-permute-done | bytes 65568 | tf_op jit(solution)/shard_map/ppermute | solution.py:26
  19.6 1.6 %collective-permute-start.6 = (bf16[256,512]{1,0:T(8,128)(2,1)S(1)}, bf16[256,512]{1,0:T(8,128)(2,1)S(1)}, u32[]{:S(2)}, u32[]{:S(2)}) collective-permute-start(bf16[256,512]{1,0:T(8,128)(2,1)S(1)} %get-tuple-element.240), channel_id=1, source_target_pairs={{0,4},{2,6},{4,0},{6,2},{8,12},{10,14},{12,8},{14,10},{16,20},{18,... | collective-permute-start | bytes 786440 | tf_op jit(solution)/shard_map/ppermute | solution.py:26
  21.4 1.5 %collective-permute-start.5 = (bf16[128,512]{1,0:T(8,128)(2,1)S(1)}, bf16[128,512]{1,0:T(8,128)(2,1)S(1)}, u32[]{:S(2)}, u32[]{:S(2)}) collective-permute-start(bf16[128,512]{1,0:T(8,128)(2,1)S(1)} %copy-done.15), channel_id=1, source_target_pairs={{0,1},{1,0},{2,3},{3,2},{4,5},{5,4},{6,7},{7,6},{8,9},{9,8},{10,11... | collective-permute-start | bytes 393224 | tf_op jit(solution)/shard_map/ppermute | solution.py:31
  22.9 3.4 %collective-permute-done.6 = bf16[256,512]{1,0:T(8,128)(2,1)S(1)} collective-permute-done((bf16[256,512]{1,0:T(8,128)(2,1)S(1)}, bf16[256,512]{1,0:T(8,128)(2,1)S(1)}, u32[]{:S(2)}, u32[]{:S(2)}) %collective-permute-start.6) | collective-permute-done | bytes 262176 | tf_op jit(solution)/shard_map/ppermute | solution.py:26
  26.3 1.6 %collective-permute-start.12 = (bf16[192,768]{1,0:T(8,128)(2,1)}, bf16[192,768]{1,0:T(8,128)(2,1)S(1)}, u32[]{:S(2)}, u32[]{:S(2)}) collective-permute-start(bf16[192,768]{1,0:T(8,128)(2,1)} %get-tuple-element.121), channel_id=1, source_target_pairs={{0,1},{1,0},{2,3},{3,2},{4,5},{5,4},{6,7},{7,6},{8,9},{9,8},{10,11... | collective-permute-start | bytes 884744 | tf_op jit(solution)/shard_map/ppermute | solution.py:31
  28.6 2.6 %collective-permute-start.10 = (bf16[64,512]{1,0:T(8,128)(2,1)S(1)}, bf16[64,512]{1,0:T(8,128)(2,1)S(1)}, u32[]{:S(2)}, u32[]{:S(2)}) collective-permute-start(bf16[64,512]{1,0:T(8,128)(2,1)S(1)} %pad_maximum_fusion.5), channel_id=1, source_target_pairs={{0,24},{2,26},{4,28},{6,30},{8,16},{10,18},{12,20},{14,22},{16,8},... | collective-permute-start | bytes 196616 | tf_op jit(solution)/shard_map/ppermute | solution.py:26
  31.2 1.3 %collective-permute-start.9 = (bf16[64,512]{1,0:T(8,128)(2,1)S(1)}, bf16[64,512]{1,0:T(8,128)(2,1)S(1)}, u32[]{:S(2)}, u32[]{:S(2)}) collective-permute-start(bf16[64,512]{1,0:T(8,128)(2,1)S(1)} %pad_maximum_fusion.5), channel_id=1, source_target_pairs={{0,16},{2,18},{4,20},{6,22},{8,24},{10,26},{12,28},{14,30},{16,0},... | collective-permute-start | bytes 196616 | tf_op jit(solution)/shard_map/ppermute | solution.py:26
  34.1 5.4 %span_attention.4 = (bf16[96,6144]{1,0:T(8,128)(2,1)}, bf16[96,6144]{1,0:T(8,128)(2,1)}, bf16[192,768]{1,0:T(8,128)(2,1)S(1)}, bf16[704,512]{1,0:T(8,128)(2,1)S(1)}, bf16[704,512]{1,0:T(8,128)(2,1)S(1)}) custom-call(s32[16,16]{1,0:T(8,128)S(1)} %copy-done.5, s32[3]{0:T(128)S(1)} %get-tuple-element.247.place, bf16[192,768]{1,0:T(8,128)(2,1)S(1)} %copy-done.7, ...), custom_call_target="tpu_custom_call" | custom-call | flops 981467136 | bytes 2359296 | tf_op jit(solution)/shard_map/span_attention/pallas_call | solution.py:243
  39.5 1.6 %collective-permute-start.13 = (bf16[192,768]{1,0:T(8,128)(2,1)S(1)}, bf16[192,768]{1,0:T(8,128)(2,1)S(1)}, u32[]{:S(2)}, u32[]{:S(2)}) collective-permute-start(bf16[192,768]{1,0:T(8,128)(2,1)S(1)} %copy-done.14), channel_id=1, source_target_pairs={{0,1},{1,0},{2,3},{3,2},{4,5},{5,4},{6,7},{7,6},{8,9},{9,8},{10,11... | collective-permute-start | bytes 884744 | tf_op jit(solution)/shard_map/ppermute | solution.py:31
  41.1 1.6 %collective-permute-start.14 = (bf16[256,512]{1,0:T(8,128)(2,1)S(1)}, bf16[256,512]{1,0:T(8,128)(2,1)S(1)}, u32[]{:S(2)}, u32[]{:S(2)}) collective-permute-start(bf16[256,512]{1,0:T(8,128)(2,1)S(1)} %get-tuple-element.234), channel_id=1, source_target_pairs={{0,4},{2,6},{4,0},{6,2},{8,12},{10,14},{12,8},{14,10},{16,20},{18,... | collective-permute-start | bytes 786440 | tf_op jit(solution)/shard_map/ppermute | solution.py:26
  42.7 5.4 %span_attention.5 = (bf16[96,6144]{1,0:T(8,128)(2,1)}, bf16[96,6144]{1,0:T(8,128)(2,1)}, bf16[192,768]{1,0:T(8,128)(2,1)S(1)}, bf16[704,512]{1,0:T(8,128)(2,1)S(1)}, bf16[704,512]{1,0:T(8,128)(2,1)S(1)}) custom-call(s32[16,16]{1,0:T(8,128)S(1)} %copy-done.5, ...), custom_call_target="tpu_custom_call", output_to_operand_aliasing={{0}: (6, {}), {1}: (7, {}), {3}: (8, {}), {4}: (9, {})} | custom-call | flops 981467136 | bytes 2359296 | tf_op jit(solution)/shard_map/span_attention/pallas_call | solution.py:243
  53.2 5.3 %span_attention.6 = (bf16[96,6144]{1,0:T(8,128)(2,1)}, bf16[96,6144]{1,0:T(8,128)(2,1)}, bf16[192,768]{1,0:T(8,128)(2,1)S(1)}, bf16[704,512]{1,0:T(8,128)(2,1)S(1)}, bf16[704,512]{1,0:T(8,128)(2,1)S(1)}) custom-call(s32[16,16]{1,0:T(8,128)S(1)} %copy-done.5, s32[3]{0:T(128)S(1)} %get-tuple-element.198.place, ...), custom_call_target="tpu_custom_call", output_to_operand_aliasing={{0}: (6, {}), {1}: (7, {})} | custom-call | flops 981467136 | bytes 2359296 | tf_op jit(solution)/shard_map/span_attention/pallas_call | solution.py:243
  58.6 1.6 %collective-permute-start.22 = (bf16[192,768]{1,0:T(8,128)(2,1)S(1)}, bf16[192,768]{1,0:T(8,128)(2,1)S(1)}, u32[]{:S(2)}, u32[]{:S(2)}) collective-permute-start(bf16[192,768]{1,0:T(8,128)(2,1)S(1)} %copy-done.9), channel_id=1, source_target_pairs={{0,1},{1,0},{2,3},{3,2},{4,5},{5,4},{6,7},{7,6},{8,9},{9,8},{10,11... | collective-permute-start | bytes 884744 | tf_op jit(solution)/shard_map/ppermute | solution.py:31
  61.7 1.1 %fusion.3 = (bf16[256,512]{1,0:T(8,128)(2,1)S(1)}, f32[256,512]{1,0:T(8,128)S(1)}) fusion(bf16[256,512]{1,0:T(8,128)(2,1)S(1)} %collective-permute-done.17, bf16[704,512]{1,0:T(8,128)(2,1)} %collective-permute-done.16, bf16[704,512]{1,0:T(8,128)(2,1)S(1)} %get-tuple-element.153), kind=kLoop, calls=%fused_computation.56 | loop fusion | flops 786432 | bytes 1572864 | tf_op jit(solution)/shard_map/convert.5
  62.8 2.5 %collective-permute-start.21 = (bf16[64,512]{1,0:T(8,128)(2,1)S(1)}, bf16[64,512]{1,0:T(8,128)(2,1)S(1)}, u32[]{:S(2)}, u32[]{:S(2)}) collective-permute-start(bf16[64,512]{1,0:T(8,128)(2,1)S(1)} %get-tuple-element.211), channel_id=1, source_target_pairs={{0,24},{2,26},{4,28},{6,30},{8,16},{10,18},{12,20},{14,22},{16,8},... | collective-permute-start | bytes 196616 | tf_op jit(solution)/shard_map/ppermute | solution.py:26
  65.6 1.7 %collective-permute-start.19 = (bf16[64,512]{1,0:T(8,128)(2,1)S(1)}, bf16[64,512]{1,0:T(8,128)(2,1)S(1)}, u32[]{:S(2)}, u32[]{:S(2)}) collective-permute-start(bf16[64,512]{1,0:T(8,128)(2,1)S(1)} %get-tuple-element.213), channel_id=1, source_target_pairs={{0,8},{2,10},{4,12},{6,14},{8,0},{10,2},{12,4},{14,6},{16,24},{18,... | collective-permute-start | bytes 196616 | tf_op jit(solution)/shard_map/ppermute | solution.py:26
  67.3 5.4 %span_attention.7 = (bf16[96,6144]{1,0:T(8,128)(2,1)}, bf16[96,6144]{1,0:T(8,128)(2,1)}, bf16[192,768]{1,0:T(8,128)(2,1)S(1)}, bf16[704,512]{1,0:T(8,128)(2,1)S(1)}, bf16[704,512]{1,0:T(8,128)(2,1)S(1)}) custom-call(s32[16,16]{1,0:T(8,128)S(1)} %copy-done.5, ...), custom_call_target="tpu_custom_call", output_to_operand_aliasing={{0}: (6, {}), {1}: (7, {}), {3}: (8, {}), {4}: (9, {})} | custom-call | flops 981467136 | bytes 2359296 | tf_op jit(solution)/shard_map/span_attention/pallas_call | solution.py:243
  72.8 1.6 %collective-permute-start.29 = (bf16[192,768]{1,0:T(8,128)(2,1)S(1)}, bf16[192,768]{1,0:T(8,128)(2,1)S(1)}, u32[]{:S(2)}, u32[]{:S(2)}) collective-permute-start(bf16[192,768]{1,0:T(8,128)(2,1)S(1)} %get-tuple-element.181), channel_id=1, source_target_pairs={{0,1},{1,0},{2,3},{3,2},{4,5},{5,4},{6,7},{7,6},{8,9},{9,8},{10,11... | collective-permute-start | bytes 884744 | tf_op jit(solution)/shard_map/ppermute | solution.py:31
  77.6 5.8 %collective-permute-done.24 = bf16[256,512]{1,0:T(8,128)(2,1)S(1)} collective-permute-done((bf16[256,512]{1,0:T(8,128)(2,1)S(1)}, bf16[256,512]{1,0:T(8,128)(2,1)S(1)}, u32[]{:S(2)}, u32[]{:S(2)}) %collective-permute-start.24) | collective-permute-done | bytes 262176 | tf_op jit(solution)/shard_map/ppermute | solution.py:26
  84.0 2.5 %collective-permute-start.27 = (bf16[64,512]{1,0:T(8,128)(2,1)S(1)}, bf16[64,512]{1,0:T(8,128)(2,1)S(1)}, u32[]{:S(2)}, u32[]{:S(2)}) collective-permute-start(bf16[64,512]{1,0:T(8,128)(2,1)S(1)} %get-tuple-element.209), channel_id=1, source_target_pairs={{0,24},{2,26},{4,28},{6,30},{8,16},{10,18},{12,20},{14,22},{16,8},... | collective-permute-start | bytes 196616 | tf_op jit(solution)/shard_map/ppermute | solution.py:26
  87.2 1.5 %collective-permute-done.25 = bf16[64,512]{1,0:T(8,128)(2,1)S(1)} collective-permute-done((bf16[64,512]{1,0:T(8,128)(2,1)S(1)}, bf16[64,512]{1,0:T(8,128)(2,1)S(1)}, u32[]{:S(2)}, u32[]{:S(2)}) %collective-permute-start.25) | collective-permute-done | bytes 65568 | tf_op jit(solution)/shard_map/ppermute | solution.py:26
  88.6 1.5 %collective-permute-start.30 = (bf16[128,512]{1,0:T(8,128)(2,1)S(1)}, bf16[128,512]{1,0:T(8,128)(2,1)S(1)}, u32[]{:S(2)}, u32[]{:S(2)}) collective-permute-start(bf16[128,512]{1,0:T(8,128)(2,1)S(1)} %pad_maximum_fusion.1), channel_id=1, source_target_pairs={{0,1},{1,0},{2,3},{3,2},{4,5},{5,4},{6,7},{7,6},{8,9},{9,8},{10,11... | collective-permute-start | bytes 393224 | tf_op jit(solution)/shard_map/ppermute | solution.py:31
  90.5 2.4 %collective-permute-done.26 = bf16[64,512]{1,0:T(8,128)(2,1)S(1)} collective-permute-done((bf16[64,512]{1,0:T(8,128)(2,1)S(1)}, bf16[64,512]{1,0:T(8,128)(2,1)S(1)}, u32[]{:S(2)}, u32[]{:S(2)}) %collective-permute-start.26) | collective-permute-done | bytes 65568 | tf_op jit(solution)/shard_map/ppermute | solution.py:26
  93.0 1.6 %collective-permute-start.31 = (bf16[128,512]{1,0:T(8,128)(2,1)S(1)}, bf16[128,512]{1,0:T(8,128)(2,1)S(1)}, u32[]{:S(2)}, u32[]{:S(2)}) collective-permute-start(bf16[128,512]{1,0:T(8,128)(2,1)S(1)} %pad_maximum_fusion.3), channel_id=1, source_target_pairs={{0,1},{1,0},{2,3},{3,2},{4,5},{5,4},{6,7},{7,6},{8,9},{9,8},{10,11... | collective-permute-start | bytes 393224 | tf_op jit(solution)/shard_map/ppermute | solution.py:31
  96.8 1.2 %collective-permute-done.31.refs_3_ = bf16[128,512]{1,0:T(8,128)(2,1)S(1)} collective-permute-done((bf16[128,512]{1,0:T(8,128)(2,1)S(1)}, bf16[128,512]{1,0:T(8,128)(2,1)S(1)}, u32[]{:S(2)}, u32[]{:S(2)}) %collective-permute-start.31) | collective-permute-done | bytes 131104 | tf_op jit(solution)/shard_map/ppermute | solution.py:31
  98.7 2.0 %unpack_gradients.1 = (bf16[96,1024]{1,0:T(8,128)(2,1)}, bf16[96,1024]{1,0:T(8,128)(2,1)}, bf16[32,1024]{1,0:T(8,128)(2,1)}, bf16[32,1024]{1,0:T(8,128)(2,1)}) custom-call(bf16[128,512]{1,0:T(8,128)(2,1)} %get-tuple-element.249.refs_0_, bf16[128,512]{1,0:T(8,128)(2,1)} %copy-done.12, bf16[128,512]{1,0:T(8,128)(2,1)} %get-tuple-element.250.refs_2_, ...), custom_call_target="tpu_custom_call" | custom-call | tf_op jit(solution)/shard_map/unpack_gradients/pallas_call | solution.py:284
  (113 shorter events, 17.8 us)
Async XLA Ops:
  2.6 6.7 %collective-permute-start = (bf16[128,512]{1,0:T(8,128)(2,1)}, bf16[128,512]{1,0:T(8,128)(2,1)S(1)}, u32[]{:S(2)}, u32[]{:S(2)}) collective-permute-start(bf16[128,512]{1,0:T(8,128)(2,1)} %get-tuple-element.103), channel_id=1, source_target_pairs={{0,1},{1,0},{2,3},{3,2},{4,5},{5,4},{6,7},{7,6},{8,9},{9,8},{10,11... | collective-permute-start | bytes 393224 | tf_op jit(solution)/shard_map/ppermute | solution.py:31
  9.4 6.0 %collective-permute-start.2 = (bf16[64,512]{1,0:T(8,128)(2,1)S(1)}, bf16[64,512]{1,0:T(8,128)(2,1)S(1)}, u32[]{:S(2)}, u32[]{:S(2)}) collective-permute-start(bf16[64,512]{1,0:T(8,128)(2,1)S(1)} %pad_maximum_fusion.4), channel_id=1, source_target_pairs={{0,8},{2,10},{4,12},{6,14},{8,0},{10,2},{12,4},{14,6},{16,24},{18,... | collective-permute-start | bytes 196616 | tf_op jit(solution)/shard_map/ppermute | solution.py:26
  11.2 8.4 %collective-permute-start.4 = (bf16[64,512]{1,0:T(8,128)(2,1)S(1)}, bf16[64,512]{1,0:T(8,128)(2,1)S(1)}, u32[]{:S(2)}, u32[]{:S(2)}) collective-permute-start(bf16[64,512]{1,0:T(8,128)(2,1)S(1)} %pad_maximum_fusion.4), channel_id=1, source_target_pairs={{0,24},{2,26},{4,28},{6,30},{8,16},{10,18},{12,20},{14,22},{16,8},... | collective-permute-start | bytes 196616 | tf_op jit(solution)/shard_map/ppermute | solution.py:26
  13.7 5.9 %collective-permute-start.3 = (bf16[64,512]{1,0:T(8,128)(2,1)S(1)}, bf16[64,512]{1,0:T(8,128)(2,1)S(1)}, u32[]{:S(2)}, u32[]{:S(2)}) collective-permute-start(bf16[64,512]{1,0:T(8,128)(2,1)S(1)} %pad_maximum_fusion.4), channel_id=1, source_target_pairs={{0,16},{2,18},{4,20},{6,22},{8,24},{10,26},{12,28},{14,30},{16,0},... | collective-permute-start | bytes 196616 | tf_op jit(solution)/shard_map/ppermute | solution.py:26
  13.8 7.5 %collective-permute-start.1 = (bf16[192,768]{1,0:T(8,128)(2,1)}, bf16[192,768]{1,0:T(8,128)(2,1)S(1)}, u32[]{:S(2)}, u32[]{:S(2)}) collective-permute-start(bf16[192,768]{1,0:T(8,128)(2,1)} %get-tuple-element.105), channel_id=1, source_target_pairs={{0,1},{1,0},{2,3},{3,2},{4,5},{5,4},{6,7},{7,6},{8,9},{9,8},{10,11... | collective-permute-start | bytes 884744 | tf_op jit(solution)/shard_map/ppermute | solution.py:31
  19.6 6.7 %collective-permute-start.6 = (bf16[256,512]{1,0:T(8,128)(2,1)S(1)}, bf16[256,512]{1,0:T(8,128)(2,1)S(1)}, u32[]{:S(2)}, u32[]{:S(2)}) collective-permute-start(bf16[256,512]{1,0:T(8,128)(2,1)S(1)} %get-tuple-element.240), channel_id=1, source_target_pairs={{0,4},{2,6},{4,0},{6,2},{8,12},{10,14},{12,8},{14,10},{16,20},{18,... | collective-permute-start | bytes 786440 | tf_op jit(solution)/shard_map/ppermute | solution.py:26
  21.4 5.0 %collective-permute-start.5 = (bf16[128,512]{1,0:T(8,128)(2,1)S(1)}, bf16[128,512]{1,0:T(8,128)(2,1)S(1)}, u32[]{:S(2)}, u32[]{:S(2)}) collective-permute-start(bf16[128,512]{1,0:T(8,128)(2,1)S(1)} %copy-done.15), channel_id=1, source_target_pairs={{0,1},{1,0},{2,3},{3,2},{4,5},{5,4},{6,7},{7,6},{8,9},{9,8},{10,11... | collective-permute-start | bytes 393224 | tf_op jit(solution)/shard_map/ppermute | solution.py:31
  26.3 13.1 %collective-permute-start.12 = (bf16[192,768]{1,0:T(8,128)(2,1)}, bf16[192,768]{1,0:T(8,128)(2,1)S(1)}, u32[]{:S(2)}, u32[]{:S(2)}) collective-permute-start(bf16[192,768]{1,0:T(8,128)(2,1)} %get-tuple-element.121), channel_id=1, source_target_pairs={{0,1},{1,0},{2,3},{3,2},{4,5},{5,4},{6,7},{7,6},{8,9},{9,8},{10,11... | collective-permute-start | bytes 884744 | tf_op jit(solution)/shard_map/ppermute | solution.py:31
  27.9 11.6 %collective-permute-start.11 = (bf16[192,768]{1,0:T(8,128)(2,1)}, bf16[192,768]{1,0:T(8,128)(2,1)S(1)}, u32[]{:S(2)}, u32[]{:S(2)}) collective-permute-start(bf16[192,768]{1,0:T(8,128)(2,1)} %get-tuple-element.113), channel_id=1, source_target_pairs={{0,1},{1,0},{2,3},{3,2},{4,5},{5,4},{6,7},{7,6},{8,9},{9,8},{10,11... | collective-permute-start | bytes 884744 | tf_op jit(solution)/shard_map/ppermute | solution.py:31
  28.4 4.1 %collective-permute-start.7 = (bf16[704,512]{1,0:T(8,128)(2,1)S(1)}, bf16[704,512]{1,0:T(8,128)(2,1)S(1)}, u32[]{:S(2)}, u32[]{:S(2)}) collective-permute-start(bf16[704,512]{1,0:T(8,128)(2,1)S(1)} %constant_dynamic-update-slice_fusion.5.refs_1_), channel_id=1, source_target_pairs={{0,2},{2,0},{4,6},{6,4},{8,10},{10,8},{12,14},{14,12},{16,18},{18,... | collective-permute-start | bytes 2162696 | tf_op jit(solution)/shard_map/ppermute | solution.py:26
  28.6 10.8 %collective-permute-start.10 = (bf16[64,512]{1,0:T(8,128)(2,1)S(1)}, bf16[64,512]{1,0:T(8,128)(2,1)S(1)}, u32[]{:S(2)}, u32[]{:S(2)}) collective-permute-start(bf16[64,512]{1,0:T(8,128)(2,1)S(1)} %pad_maximum_fusion.5), channel_id=1, source_target_pairs={{0,24},{2,26},{4,28},{6,30},{8,16},{10,18},{12,20},{14,22},{16,8},... | collective-permute-start | bytes 196616 | tf_op jit(solution)/shard_map/ppermute | solution.py:26
  31.2 8.2 %collective-permute-start.9 = (bf16[64,512]{1,0:T(8,128)(2,1)S(1)}, bf16[64,512]{1,0:T(8,128)(2,1)S(1)}, u32[]{:S(2)}, u32[]{:S(2)}) collective-permute-start(bf16[64,512]{1,0:T(8,128)(2,1)S(1)} %pad_maximum_fusion.5), channel_id=1, source_target_pairs={{0,16},{2,18},{4,20},{6,22},{8,24},{10,26},{12,28},{14,30},{16,0},... | collective-permute-start | bytes 196616 | tf_op jit(solution)/shard_map/ppermute | solution.py:26
  32.5 6.9 %collective-permute-start.8 = (bf16[64,512]{1,0:T(8,128)(2,1)S(1)}, bf16[64,512]{1,0:T(8,128)(2,1)S(1)}, u32[]{:S(2)}, u32[]{:S(2)}) collective-permute-start(bf16[64,512]{1,0:T(8,128)(2,1)S(1)} %pad_maximum_fusion.5), channel_id=1, source_target_pairs={{0,8},{2,10},{4,12},{6,14},{8,0},{10,2},{12,4},{14,6},{16,24},{18,... | collective-permute-start | bytes 196616 | tf_op jit(solution)/shard_map/ppermute | solution.py:26
  39.5 9.3 %collective-permute-start.13 = (bf16[192,768]{1,0:T(8,128)(2,1)S(1)}, bf16[192,768]{1,0:T(8,128)(2,1)S(1)}, u32[]{:S(2)}, u32[]{:S(2)}) collective-permute-start(bf16[192,768]{1,0:T(8,128)(2,1)S(1)} %copy-done.14), channel_id=1, source_target_pairs={{0,1},{1,0},{2,3},{3,2},{4,5},{5,4},{6,7},{7,6},{8,9},{9,8},{10,11... | collective-permute-start | bytes 884744 | tf_op jit(solution)/shard_map/ppermute | solution.py:31
  41.1 7.9 %collective-permute-start.14 = (bf16[256,512]{1,0:T(8,128)(2,1)S(1)}, bf16[256,512]{1,0:T(8,128)(2,1)S(1)}, u32[]{:S(2)}, u32[]{:S(2)}) collective-permute-start(bf16[256,512]{1,0:T(8,128)(2,1)S(1)} %get-tuple-element.234), channel_id=1, source_target_pairs={{0,4},{2,6},{4,0},{6,2},{8,12},{10,14},{12,8},{14,10},{16,20},{18,... | collective-permute-start | bytes 786440 | tf_op jit(solution)/shard_map/ppermute | solution.py:26
  48.8 2.3 %collective-permute-start.16 = (bf16[704,512]{1,0:T(8,128)(2,1)S(1)}, bf16[704,512]{1,0:T(8,128)(2,1)}, u32[]{:S(2)}, u32[]{:S(2)}) collective-permute-start(bf16[704,512]{1,0:T(8,128)(2,1)S(1)} %get-tuple-element.150), channel_id=1, source_target_pairs={{0,2},{2,0},{4,6},{6,4},{8,10},{10,8},{12,14},{14,12},{16,18},{18,... | collective-permute-start | bytes 2162696 | tf_op jit(solution)/shard_map/ppermute | solution.py:26
  49.5 3.7 %collective-permute-start.15 = (bf16[704,512]{1,0:T(8,128)(2,1)S(1)}, bf16[704,512]{1,0:T(8,128)(2,1)S(1)}, u32[]{:S(2)}, u32[]{:S(2)}) collective-permute-start(bf16[704,512]{1,0:T(8,128)(2,1)S(1)} %constant_dynamic-update-slice_fusion.16.refs_1_), channel_id=1, source_target_pairs={{0,2},{2,0},{4,6},{6,4},{8,10},{10,8},{12,14},{14,12},{16,18},{18,... | collective-permute-start | bytes 2162696 | tf_op jit(solution)/shard_map/ppermute | solution.py:26
  49.5 12.2 %collective-permute-start.18 = (bf16[192,768]{1,0:T(8,128)(2,1)}, bf16[192,768]{1,0:T(8,128)(2,1)S(1)}, u32[]{:S(2)}, u32[]{:S(2)}) collective-permute-start(bf16[192,768]{1,0:T(8,128)(2,1)} %copy-done.6), channel_id=1, source_target_pairs={{0,1},{1,0},{2,3},{3,2},{4,5},{5,4},{6,7},{7,6},{8,9},{9,8},{10,11... | collective-permute-start | bytes 884744 | tf_op jit(solution)/shard_map/ppermute | solution.py:31
  52.1 9.6 %collective-permute-start.17 = (bf16[256,512]{1,0:T(8,128)(2,1)S(1)}, bf16[256,512]{1,0:T(8,128)(2,1)S(1)}, u32[]{:S(2)}, u32[]{:S(2)}) collective-permute-start(bf16[256,512]{1,0:T(8,128)(2,1)S(1)} %add_convert_fusion.1), channel_id=1, source_target_pairs={{0,4},{2,6},{4,0},{6,2},{8,12},{10,14},{12,8},{14,10},{16,20},{18,... | collective-permute-start | bytes 786440 | tf_op jit(solution)/shard_map/ppermute | solution.py:26
  58.6 14.1 %collective-permute-start.22 = (bf16[192,768]{1,0:T(8,128)(2,1)S(1)}, bf16[192,768]{1,0:T(8,128)(2,1)S(1)}, u32[]{:S(2)}, u32[]{:S(2)}) collective-permute-start(bf16[192,768]{1,0:T(8,128)(2,1)S(1)} %copy-done.9), channel_id=1, source_target_pairs={{0,1},{1,0},{2,3},{3,2},{4,5},{5,4},{6,7},{7,6},{8,9},{9,8},{10,11... | collective-permute-start | bytes 884744 | tf_op jit(solution)/shard_map/ppermute | solution.py:31
  60.2 32.8 %collective-permute-start.28 = (bf16[192,768]{1,0:T(8,128)(2,1)S(1)}, bf16[192,768]{1,0:T(8,128)(2,1)S(1)}, u32[]{:S(2)}, u32[]{:S(2)}) collective-permute-start(bf16[192,768]{1,0:T(8,128)(2,1)S(1)} %get-tuple-element.180), channel_id=1, source_target_pairs={{0,1},{1,0},{2,3},{3,2},{4,5},{5,4},{6,7},{7,6},{8,9},{9,8},{10,11... | collective-permute-start | bytes 884744 | tf_op jit(solution)/shard_map/ppermute | solution.py:31
  62.8 9.9 %collective-permute-start.21 = (bf16[64,512]{1,0:T(8,128)(2,1)S(1)}, bf16[64,512]{1,0:T(8,128)(2,1)S(1)}, u32[]{:S(2)}, u32[]{:S(2)}) collective-permute-start(bf16[64,512]{1,0:T(8,128)(2,1)S(1)} %get-tuple-element.211), channel_id=1, source_target_pairs={{0,24},{2,26},{4,28},{6,30},{8,16},{10,18},{12,20},{14,22},{16,8},... | collective-permute-start | bytes 196616 | tf_op jit(solution)/shard_map/ppermute | solution.py:26
  65.4 7.3 %collective-permute-start.20 = (bf16[64,512]{1,0:T(8,128)(2,1)S(1)}, bf16[64,512]{1,0:T(8,128)(2,1)S(1)}, u32[]{:S(2)}, u32[]{:S(2)}) collective-permute-start(bf16[64,512]{1,0:T(8,128)(2,1)S(1)} %get-tuple-element.212), channel_id=1, source_target_pairs={{0,16},{2,18},{4,20},{6,22},{8,24},{10,26},{12,28},{14,30},{16,0},... | collective-permute-start | bytes 196616 | tf_op jit(solution)/shard_map/ppermute | solution.py:26
  65.6 7.1 %collective-permute-start.19 = (bf16[64,512]{1,0:T(8,128)(2,1)S(1)}, bf16[64,512]{1,0:T(8,128)(2,1)S(1)}, u32[]{:S(2)}, u32[]{:S(2)}) collective-permute-start(bf16[64,512]{1,0:T(8,128)(2,1)S(1)} %get-tuple-element.213), channel_id=1, source_target_pairs={{0,8},{2,10},{4,12},{6,14},{8,0},{10,2},{12,4},{14,6},{16,24},{18,... | collective-permute-start | bytes 196616 | tf_op jit(solution)/shard_map/ppermute | solution.py:26
  72.7 2.3 %collective-permute-start.23 = (bf16[704,512]{1,0:T(8,128)(2,1)S(1)}, bf16[704,512]{1,0:T(8,128)(2,1)S(1)}, u32[]{:S(2)}, u32[]{:S(2)}) collective-permute-start(bf16[704,512]{1,0:T(8,128)(2,1)S(1)} %get-tuple-element.177), channel_id=1, source_target_pairs={{0,2},{2,0},{4,6},{6,4},{8,10},{10,8},{12,14},{14,12},{16,18},{18,... | collective-permute-start | bytes 2162696 | tf_op jit(solution)/shard_map/ppermute | solution.py:26
  72.8 20.1 %collective-permute-start.29 = (bf16[192,768]{1,0:T(8,128)(2,1)S(1)}, bf16[192,768]{1,0:T(8,128)(2,1)S(1)}, u32[]{:S(2)}, u32[]{:S(2)}) collective-permute-start(bf16[192,768]{1,0:T(8,128)(2,1)S(1)} %get-tuple-element.181), channel_id=1, source_target_pairs={{0,1},{1,0},{2,3},{3,2},{4,5},{5,4},{6,7},{7,6},{8,9},{9,8},{10,11... | collective-permute-start | bytes 884744 | tf_op jit(solution)/shard_map/ppermute | solution.py:31
  75.1 8.4 %collective-permute-start.24 = (bf16[256,512]{1,0:T(8,128)(2,1)S(1)}, bf16[256,512]{1,0:T(8,128)(2,1)S(1)}, u32[]{:S(2)}, u32[]{:S(2)}) collective-permute-start(bf16[256,512]{1,0:T(8,128)(2,1)S(1)} %add_convert_fusion), channel_id=1, source_target_pairs={{0,4},{2,6},{4,0},{6,2},{8,12},{10,14},{12,8},{14,10},{16,20},{18,... | collective-permute-start | bytes 786440 | tf_op jit(solution)/shard_map/ppermute | solution.py:26
  83.6 5.0 %collective-permute-start.25 = (bf16[64,512]{1,0:T(8,128)(2,1)S(1)}, bf16[64,512]{1,0:T(8,128)(2,1)S(1)}, u32[]{:S(2)}, u32[]{:S(2)}) collective-permute-start(bf16[64,512]{1,0:T(8,128)(2,1)S(1)} %get-tuple-element.208), channel_id=1, source_target_pairs={{0,8},{2,10},{4,12},{6,14},{8,0},{10,2},{12,4},{14,6},{16,24},{18,... | collective-permute-start | bytes 196616 | tf_op jit(solution)/shard_map/ppermute | solution.py:26
  84.0 6.5 %collective-permute-start.27 = (bf16[64,512]{1,0:T(8,128)(2,1)S(1)}, bf16[64,512]{1,0:T(8,128)(2,1)S(1)}, u32[]{:S(2)}, u32[]{:S(2)}) collective-permute-start(bf16[64,512]{1,0:T(8,128)(2,1)S(1)} %get-tuple-element.209), channel_id=1, source_target_pairs={{0,24},{2,26},{4,28},{6,30},{8,16},{10,18},{12,20},{14,22},{16,8},... | collective-permute-start | bytes 196616 | tf_op jit(solution)/shard_map/ppermute | solution.py:26
  86.5 6.4 %collective-permute-start.26 = (bf16[64,512]{1,0:T(8,128)(2,1)S(1)}, bf16[64,512]{1,0:T(8,128)(2,1)S(1)}, u32[]{:S(2)}, u32[]{:S(2)}) collective-permute-start(bf16[64,512]{1,0:T(8,128)(2,1)S(1)} %get-tuple-element.210), channel_id=1, source_target_pairs={{0,16},{2,18},{4,20},{6,22},{8,24},{10,26},{12,28},{14,30},{16,0},... | collective-permute-start | bytes 196616 | tf_op jit(solution)/shard_map/ppermute | solution.py:26
  88.6 8.2 %collective-permute-start.30 = (bf16[128,512]{1,0:T(8,128)(2,1)S(1)}, bf16[128,512]{1,0:T(8,128)(2,1)S(1)}, u32[]{:S(2)}, u32[]{:S(2)}) collective-permute-start(bf16[128,512]{1,0:T(8,128)(2,1)S(1)} %pad_maximum_fusion.1), channel_id=1, source_target_pairs={{0,1},{1,0},{2,3},{3,2},{4,5},{5,4},{6,7},{7,6},{8,9},{9,8},{10,11... | collective-permute-start | bytes 393224 | tf_op jit(solution)/shard_map/ppermute | solution.py:31
  93.0 5.0 %collective-permute-start.31 = (bf16[128,512]{1,0:T(8,128)(2,1)S(1)}, bf16[128,512]{1,0:T(8,128)(2,1)S(1)}, u32[]{:S(2)}, u32[]{:S(2)}) collective-permute-start(bf16[128,512]{1,0:T(8,128)(2,1)S(1)} %pad_maximum_fusion.3), channel_id=1, source_target_pairs={{0,1},{1,0},{2,3},{3,2},{4,5},{5,4},{6,7},{7,6},{8,9},{9,8},{10,11... | collective-permute-start | bytes 393224 | tf_op jit(solution)/shard_map/ppermute | solution.py:31
  (16 other events, 111.9 us)

commit v2 on v0

--- a/solution.py
+++ b/solution.py
@@ -18,7 +18,7 @@
 
 NEG_FILL = -1e30
 SLICE_ROWS = 256
-KERNEL_VMEM = 32 * 2**20
+KERNEL_VMEM = 16 * 2**20
 
 
 def flipped(block, bits):
@@ -464,8 +464,9 @@
                 sent.append([shifted(block, -step) for step, block in zip(steps, block_set)])
         if waiting and not last:
             noisy_sum, line = summed(*waiting[0])
-            line, outputs, sent[0] = together((line, outputs, sent[0]))
+            line, outputs = together((line, outputs))
             waiting[0] = (noisy_sum, *halved(line))
+            outputs, sent[0] = together((outputs, sent[0]))
         if last:
             if waiting:
                 waiting[0], pair, sent[:half] = together((waiting[0], pair, sent[:half]))

time: 98.1 us -> 96.9 us (0.988)
  waiting for transfers between devices: 22.4 us -> 20.7 us
    ppermute x12, waiting for transfers between devices: 5.85 us -> 4.56 us  [shifted(): lax.ppermute(block, 'head', [(i, (i + step) % count) for i in range(count)])]
    ppermute x20, starting transfers between devices: 21.7 us -> 22.8 us  [flipped(): return lax.ppermute(block, 'ctx', [(i, i ^ bits) for i in range(count)])]
  transfers between devices with their start and end apart: 32 -> 32, of which waited for: 13 -> 14; matrix products, arithmetic and copies ran while one was open for 6% -> 6% of each run, Pallas kernels for 25% -> 25%
where the time goes in v2:
time: 96.9 us; the launch traced here: 96.7 us
  starting transfers between devices  38.9 us (40%)
  Pallas kernels  28.6 us (30%)
  waiting for transfers between devices  20.7 us (21%)
  local copies, waits for them, and re-layouts  4.85 us (5%)
  other arithmetic  2.57 us (3%)
  between operations  1.1 us (1%)
    ppermute x20, starting transfers between devices, flipped(): return lax.ppermute(block, 'ctx', [(i, i ^ bits) for i in range(count)])  22.8 us
    pallas_call x4, Pallas kernels, attention(): pl.pallas_call(functools.partial(attention_kernel, shape, column, len(kep...  21.5 us
    ppermute x20, waiting for transfers between devices, flipped(): return lax.ppermute(block, 'ctx', [(i, i ^ bits) for i in range(count)])  16.2 us
    ppermute x12, starting transfers between devices, shifted(): lax.ppermute(block, 'head', [(i, (i + step) % count) for i in range(count)])  16.1 us
    ppermute x12, waiting for transfers between devices, shifted(): lax.ppermute(block, 'head', [(i, (i + step) % count) for i in range(count)])  4.56 us
    pallas_call x1, Pallas kernels, query_blocks(): pl.pallas_call(functools.partial(stack_kernel, head_count), in_specs=[vme...  3.17 us
    dynamic_update_slice x4, local copies, waits for them, and re-layouts, shards(): lax.dynamic_update_slice_in_dim(query_grad, block[rows:], start, 1)  2.91 us
    pallas_call x1, Pallas kernels, packed(): pl.pallas_call(functools.partial(pack_kernel, head_count, groups), in_spe...  1.97 us
  transfers between devices with their start and end apart: 32, of which 14 were waited for; matrix products, arithmetic and copies ran while one was open for 6% of the time, Pallas kernels for 25%

profile of v2, /device:TPU:0, one launch (start us, length us, event | category | flops | bytes accessed | tf_op | source)
XLA Modules:
  0.0 96.7 jit_solution(11237523917995293085)
XLA Ops:
  0.6 2.0 %pack_keys_values.1 = (bf16[128,512]{1,0:T(8,128)(2,1)}, bf16[128,512]{1,0:T(8,128)(2,1)}, bf16[128,512]{1,0:T(8,128)(2,1)}, bf16[128,512]{1,0:T(8,128)(2,1)}) custom-call(bf16[96,1024]{1,0:T(8,128)(2,1)} %k_noisy.1, bf16[96,1024]{1,0:T(8,128)(2,1)} %v_noisy.1, bf16[32,1024]{1,0:T(8,128)(2,1)} %k_clean.1, bf16[32,1024]{1,0:T(8,128)(2,1)} %v_clean.1), custom_call_target="tpu_custom_call" | custom-call | tf_op jit(solution)/shard_map/pack_keys_values/pallas_call | solution.py:68
  2.6 3.0 %collective-permute-start = (bf16[128,512]{1,0:T(8,128)(2,1)}, bf16[128,512]{1,0:T(8,128)(2,1)S(1)}, u32[]{:S(2)}, u32[]{:S(2)}) collective-permute-start(bf16[128,512]{1,0:T(8,128)(2,1)} %get-tuple-element.105), channel_id=1, source_target_pairs={{0,1},{1,0},{2,3},{3,2},{4,5},{5,4},{6,7},{7,6},{8,9},{9,8},{10,11... | collective-permute-start | bytes 393224 | tf_op jit(solution)/shard_map/ppermute | solution.py:31
  5.6 3.2 %stack_queries.1 = (bf16[192,768]{1,0:T(8,128)(2,1)}, bf16[192,768]{1,0:T(8,128)(2,1)}, bf16[192,768]{1,0:T(8,128)(2,1)}, bf16[192,768]{1,0:T(8,128)(2,1)}, bf16...) custom-call(bf16[96,6144]{1,0:T(8,128)(2,1)} %q.1, ...), custom_call_target="tpu_custom_call" | custom-call | tf_op jit(solution)/shard_map/stack_queries/pallas_call | solution.py:93
  9.4 1.9 %collective-permute-start.2 = (bf16[64,512]{1,0:T(8,128)(2,1)S(1)}, bf16[64,512]{1,0:T(8,128)(2,1)S(1)}, u32[]{:S(2)}, u32[]{:S(2)}) collective-permute-start(bf16[64,512]{1,0:T(8,128)(2,1)S(1)} %pad_maximum_fusion.4), channel_id=1, source_target_pairs={{0,8},{2,10},{4,12},{6,14},{8,0},{10,2},{12,4},{14,6},{16,24},{18,... | collective-permute-start | bytes 196616 | tf_op jit(solution)/shard_map/ppermute | solution.py:26
  11.2 2.5 %collective-permute-start.4 = (bf16[64,512]{1,0:T(8,128)(2,1)S(1)}, bf16[64,512]{1,0:T(8,128)(2,1)S(1)}, u32[]{:S(2)}, u32[]{:S(2)}) collective-permute-start(bf16[64,512]{1,0:T(8,128)(2,1)S(1)} %pad_maximum_fusion.4), channel_id=1, source_target_pairs={{0,24},{2,26},{4,28},{6,30},{8,16},{10,18},{12,20},{14,22},{16,8},... | collective-permute-start | bytes 196616 | tf_op jit(solution)/shard_map/ppermute | solution.py:26
  13.8 1.5 %collective-permute-start.1 = (bf16[192,768]{1,0:T(8,128)(2,1)}, bf16[192,768]{1,0:T(8,128)(2,1)S(1)}, u32[]{:S(2)}, u32[]{:S(2)}) collective-permute-start(bf16[192,768]{1,0:T(8,128)(2,1)} %get-tuple-element.107), channel_id=1, source_target_pairs={{0,1},{1,0},{2,3},{3,2},{4,5},{5,4},{6,7},{7,6},{8,9},{9,8},{10,11... | collective-permute-start | bytes 884744 | tf_op jit(solution)/shard_map/ppermute | solution.py:31
  15.4 4.2 %collective-permute-done.3 = bf16[64,512]{1,0:T(8,128)(2,1)S(1)} collective-permute-done((bf16[64,512]{1,0:T(8,128)(2,1)S(1)}, bf16[64,512]{1,0:T(8,128)(2,1)S(1)}, u32[]{:S(2)}, u32[]{:S(2)}) %collective-permute-start.3) | collective-permute-done | bytes 65568 | tf_op jit(solution)/shard_map/ppermute | solution.py:26
  19.6 1.6 %collective-permute-start.6 = (bf16[256,512]{1,0:T(8,128)(2,1)S(1)}, bf16[256,512]{1,0:T(8,128)(2,1)S(1)}, u32[]{:S(2)}, u32[]{:S(2)}) collective-permute-start(bf16[256,512]{1,0:T(8,128)(2,1)S(1)} %get-tuple-element.246), channel_id=1, source_target_pairs={{0,4},{2,6},{4,0},{6,2},{8,12},{10,14},{12,8},{14,10},{16,20},{18,... | collective-permute-start | bytes 786440 | tf_op jit(solution)/shard_map/ppermute | solution.py:26
  21.4 1.5 %collective-permute-start.5 = (bf16[128,512]{1,0:T(8,128)(2,1)S(1)}, bf16[128,512]{1,0:T(8,128)(2,1)S(1)}, u32[]{:S(2)}, u32[]{:S(2)}) collective-permute-start(bf16[128,512]{1,0:T(8,128)(2,1)S(1)} %copy-done.17), channel_id=1, source_target_pairs={{0,1},{1,0},{2,3},{3,2},{4,5},{5,4},{6,7},{7,6},{8,9},{9,8},{10,11... | collective-permute-start | bytes 393224 | tf_op jit(solution)/shard_map/ppermute | solution.py:31
  23.0 3.4 %collective-permute-done.6 = bf16[256,512]{1,0:T(8,128)(2,1)S(1)} collective-permute-done((bf16[256,512]{1,0:T(8,128)(2,1)S(1)}, bf16[256,512]{1,0:T(8,128)(2,1)S(1)}, u32[]{:S(2)}, u32[]{:S(2)}) %collective-permute-start.6) | collective-permute-done | bytes 262176 | tf_op jit(solution)/shard_map/ppermute | solution.py:26
  26.4 1.6 %collective-permute-start.12 = (bf16[192,768]{1,0:T(8,128)(2,1)S(1)}, bf16[192,768]{1,0:T(8,128)(2,1)S(1)}, u32[]{:S(2)}, u32[]{:S(2)}) collective-permute-start(bf16[192,768]{1,0:T(8,128)(2,1)S(1)} %copy-done.16), channel_id=1, source_target_pairs={{0,1},{1,0},{2,3},{3,2},{4,5},{5,4},{6,7},{7,6},{8,9},{9,8},{10,11... | collective-permute-start | bytes 884744 | tf_op jit(solution)/shard_map/ppermute | solution.py:31
  28.6 2.6 %collective-permute-start.10 = (bf16[64,512]{1,0:T(8,128)(2,1)S(1)}, bf16[64,512]{1,0:T(8,128)(2,1)S(1)}, u32[]{:S(2)}, u32[]{:S(2)}) collective-permute-start(bf16[64,512]{1,0:T(8,128)(2,1)S(1)} %pad_maximum_fusion.5), channel_id=1, source_target_pairs={{0,24},{2,26},{4,28},{6,30},{8,16},{10,18},{12,20},{14,22},{16,8},... | collective-permute-start | bytes 196616 | tf_op jit(solution)/shard_map/ppermute | solution.py:26
  31.2 1.5 %collective-permute-start.9 = (bf16[64,512]{1,0:T(8,128)(2,1)S(1)}, bf16[64,512]{1,0:T(8,128)(2,1)S(1)}, u32[]{:S(2)}, u32[]{:S(2)}) collective-permute-start(bf16[64,512]{1,0:T(8,128)(2,1)S(1)} %pad_maximum_fusion.5), channel_id=1, source_target_pairs={{0,16},{2,18},{4,20},{6,22},{8,24},{10,26},{12,28},{14,30},{16,0},... | collective-permute-start | bytes 196616 | tf_op jit(solution)/shard_map/ppermute | solution.py:26
  33.4 5.4 %span_attention.4 = (bf16[96,6144]{1,0:T(8,128)(2,1)}, bf16[96,6144]{1,0:T(8,128)(2,1)}, bf16[192,768]{1,0:T(8,128)(2,1)S(1)}, bf16[704,512]{1,0:T(8,128)(2,1)S(1)}, bf16[704,512]{1,0:T(8,128)(2,1)S(1)}) custom-call(s32[16,16]{1,0:T(8,128)S(1)} %copy-done.3, s32[3]{0:T(128)S(1)} %get-tuple-element.253.place, bf16[192,768]{1,0:T(8,128)(2,1)S(1)} %copy-done.4, ...), custom_call_target="tpu_custom_call" | custom-call | flops 981467136 | bytes 2359296 | tf_op jit(solution)/shard_map/span_attention/pallas_call | solution.py:243
  39.3 1.6 %collective-permute-start.14 = (bf16[256,512]{1,0:T(8,128)(2,1)S(1)}, bf16[256,512]{1,0:T(8,128)(2,1)S(1)}, u32[]{:S(2)}, u32[]{:S(2)}) collective-permute-start(bf16[256,512]{1,0:T(8,128)(2,1)S(1)} %get-tuple-element.240), channel_id=1, source_target_pairs={{0,4},{2,6},{4,0},{6,2},{8,12},{10,14},{12,8},{14,10},{16,20},{18,... | collective-permute-start | bytes 786440 | tf_op jit(solution)/shard_map/ppermute | solution.py:26
  40.8 1.5 %collective-permute-start.13 = (bf16[192,768]{1,0:T(8,128)(2,1)S(1)}, bf16[192,768]{1,0:T(8,128)(2,1)S(1)}, u32[]{:S(2)}, u32[]{:S(2)}) collective-permute-start(bf16[192,768]{1,0:T(8,128)(2,1)S(1)} %copy-done.14), channel_id=1, source_target_pairs={{0,1},{1,0},{2,3},{3,2},{4,5},{5,4},{6,7},{7,6},{8,9},{9,8},{10,11... | collective-permute-start | bytes 884744 | tf_op jit(solution)/shard_map/ppermute | solution.py:31
  42.3 5.4 %span_attention.5 = (bf16[96,6144]{1,0:T(8,128)(2,1)}, bf16[96,6144]{1,0:T(8,128)(2,1)}, bf16[192,768]{1,0:T(8,128)(2,1)S(1)}, bf16[704,512]{1,0:T(8,128)(2,1)S(1)}, bf16[704,512]{1,0:T(8,128)(2,1)S(1)}) custom-call(s32[16,16]{1,0:T(8,128)S(1)} %copy-done.3, ...), custom_call_target="tpu_custom_call", output_to_operand_aliasing={{0}: (6, {}), {1}: (7, {}), {3}: (8, {}), {4}: (9, {})} | custom-call | flops 981467136 | bytes 2359296 | tf_op jit(solution)/shard_map/span_attention/pallas_call | solution.py:243
  47.8 1.7 %collective-permute-done.13.refs_0_ = bf16[192,768]{1,0:T(8,128)(2,1)S(1)} collective-permute-done((bf16[192,768]{1,0:T(8,128)(2,1)S(1)}, bf16[192,768]{1,0:T(8,128)(2,1)S(1)}, u32[]{:S(2)}, u32[]{:S(2)}) %collective-permute-start.13) | collective-permute-done | bytes 294944 | tf_op jit(solution)/shard_map/ppermute | solution.py:31
  49.5 1.5 %collective-permute-start.17 = (bf16[192,768]{1,0:T(8,128)(2,1)S(1)}, bf16[192,768]{1,0:T(8,128)(2,1)S(1)}, u32[]{:S(2)}, u32[]{:S(2)}) collective-permute-start(bf16[192,768]{1,0:T(8,128)(2,1)S(1)} %get-tuple-element.164), channel_id=1, source_target_pairs={{0,1},{1,0},{2,3},{3,2},{4,5},{5,4},{6,7},{7,6},{8,9},{9,8},{10,11... | collective-permute-start | bytes 884744 | tf_op jit(solution)/shard_map/ppermute | solution.py:31
  51.0 5.4 %span_attention.6 = (bf16[96,6144]{1,0:T(8,128)(2,1)}, bf16[96,6144]{1,0:T(8,128)(2,1)}, bf16[192,768]{1,0:T(8,128)(2,1)S(1)}, bf16[704,512]{1,0:T(8,128)(2,1)S(1)}, bf16[704,512]{1,0:T(8,128)(2,1)S(1)}) custom-call(s32[16,16]{1,0:T(8,128)S(1)} %copy-done.3, s32[3]{0:T(128)S(1)} %get-tuple-element.202.place, ...), custom_call_target="tpu_custom_call", output_to_operand_aliasing={{0}: (6, {}), {1}: (7, {})} | custom-call | flops 981467136 | bytes 2359296 | tf_op jit(solution)/shard_map/span_attention/pallas_call | solution.py:243
  57.3 1.4 %collective-permute-start.18 = (bf16[256,512]{1,0:T(8,128)(2,1)S(1)}, bf16[256,512]{1,0:T(8,128)(2,1)S(1)}, u32[]{:S(2)}, u32[]{:S(2)}) collective-permute-start(bf16[256,512]{1,0:T(8,128)(2,1)S(1)} %slice.223), channel_id=1, source_target_pairs={{0,4},{2,6},{4,0},{6,2},{8,12},{10,14},{12,8},{14,10},{16,20},{18,... | collective-permute-start | bytes 786440 | tf_op jit(solution)/shard_map/ppermute | solution.py:26
  58.9 5.4 %span_attention.7 = (bf16[96,6144]{1,0:T(8,128)(2,1)}, bf16[96,6144]{1,0:T(8,128)(2,1)}, bf16[192,768]{1,0:T(8,128)(2,1)S(1)}, bf16[704,512]{1,0:T(8,128)(2,1)S(1)}, bf16[704,512]{1,0:T(8,128)(2,1)S(1)}) custom-call(s32[16,16]{1,0:T(8,128)S(1)} %copy-done.3, ...), custom_call_target="tpu_custom_call", output_to_operand_aliasing={{0}: (6, {}), {1}: (7, {}), {3}: (8, {}), {4}: (9, {})} | custom-call | flops 981467136 | bytes 2359296 | tf_op jit(solution)/shard_map/span_attention/pallas_call | solution.py:243
  64.3 1.2 %collective-permute-done.18 = bf16[256,512]{1,0:T(8,128)(2,1)S(1)} collective-permute-done((bf16[256,512]{1,0:T(8,128)(2,1)S(1)}, bf16[256,512]{1,0:T(8,128)(2,1)S(1)}, u32[]{:S(2)}, u32[]{:S(2)}) %collective-permute-start.18) | collective-permute-done | bytes 262176 | tf_op jit(solution)/shard_map/ppermute | solution.py:26
  66.4 1.5 %collective-permute-start.28 = (bf16[192,768]{1,0:T(8,128)(2,1)S(1)}, bf16[192,768]{1,0:T(8,128)(2,1)S(1)}, u32[]{:S(2)}, u32[]{:S(2)}) collective-permute-start(bf16[192,768]{1,0:T(8,128)(2,1)S(1)} %get-tuple-element.184), channel_id=1, source_target_pairs={{0,1},{1,0},{2,3},{3,2},{4,5},{5,4},{6,7},{7,6},{8,9},{9,8},{10,11... | collective-permute-start | bytes 884744 | tf_op jit(solution)/shard_map/ppermute | solution.py:31
  70.2 2.8 %collective-permute-start.24 = (bf16[64,512]{1,0:T(8,128)(2,1)S(1)}, bf16[64,512]{1,0:T(8,128)(2,1)S(1)}, u32[]{:S(2)}, u32[]{:S(2)}) collective-permute-start(bf16[64,512]{1,0:T(8,128)(2,1)S(1)} %get-tuple-element.219), channel_id=1, source_target_pairs={{0,24},{2,26},{4,28},{6,30},{8,16},{10,18},{12,20},{14,22},{16,8},... | collective-permute-start | bytes 196616 | tf_op jit(solution)/shard_map/ppermute | solution.py:26
  73.0 1.7 %collective-permute-start.22 = (bf16[64,512]{1,0:T(8,128)(2,1)S(1)}, bf16[64,512]{1,0:T(8,128)(2,1)S(1)}, u32[]{:S(2)}, u32[]{:S(2)}) collective-permute-start(bf16[64,512]{1,0:T(8,128)(2,1)S(1)} %get-tuple-element.221), channel_id=1, source_target_pairs={{0,8},{2,10},{4,12},{6,14},{8,0},{10,2},{12,4},{14,6},{16,24},{18,... | collective-permute-start | bytes 196616 | tf_op jit(solution)/shard_map/ppermute | solution.py:26
  74.7 2.1 %collective-permute-done.24 = bf16[64,512]{1,0:T(8,128)(2,1)S(1)} collective-permute-done((bf16[64,512]{1,0:T(8,128)(2,1)S(1)}, bf16[64,512]{1,0:T(8,128)(2,1)S(1)}, u32[]{:S(2)}, u32[]{:S(2)}) %collective-permute-start.24) | collective-permute-done | bytes 65568 | tf_op jit(solution)/shard_map/ppermute | solution.py:26
  80.0 1.9 %collective-permute-start.27 = (bf16[64,512]{1,0:T(8,128)(2,1)S(1)}, bf16[64,512]{1,0:T(8,128)(2,1)S(1)}, u32[]{:S(2)}, u32[]{:S(2)}) collective-permute-start(bf16[64,512]{1,0:T(8,128)(2,1)S(1)} %get-tuple-element.217), channel_id=1, source_target_pairs={{0,24},{2,26},{4,28},{6,30},{8,16},{10,18},{12,20},{14,22},{16,8},... | collective-permute-start | bytes 196616 | tf_op jit(solution)/shard_map/ppermute | solution.py:26
  85.1 1.4 %collective-permute-done.27 = bf16[64,512]{1,0:T(8,128)(2,1)S(1)} collective-permute-done((bf16[64,512]{1,0:T(8,128)(2,1)S(1)}, bf16[64,512]{1,0:T(8,128)(2,1)S(1)}, u32[]{:S(2)}, u32[]{:S(2)}) %collective-permute-start.27) | collective-permute-done | bytes 65568 | tf_op jit(solution)/shard_map/ppermute | solution.py:26
  86.5 2.3 %collective-permute-done.26 = bf16[64,512]{1,0:T(8,128)(2,1)S(1)} collective-permute-done((bf16[64,512]{1,0:T(8,128)(2,1)S(1)}, bf16[64,512]{1,0:T(8,128)(2,1)S(1)}, u32[]{:S(2)}, u32[]{:S(2)}) %collective-permute-start.26) | collective-permute-done | bytes 65568 | tf_op jit(solution)/shard_map/ppermute | solution.py:26
  92.0 2.1 %collective-permute-done.31.refs_3_ = bf16[128,512]{1,0:T(8,128)(2,1)S(1)} collective-permute-done((bf16[128,512]{1,0:T(8,128)(2,1)S(1)}, bf16[128,512]{1,0:T(8,128)(2,1)S(1)}, u32[]{:S(2)}, u32[]{:S(2)}) %collective-permute-start.31) | collective-permute-done | bytes 131104 | tf_op jit(solution)/shard_map/ppermute | solution.py:31
  94.7 2.0 %unpack_gradients.1 = (bf16[96,1024]{1,0:T(8,128)(2,1)}, bf16[96,1024]{1,0:T(8,128)(2,1)}, bf16[32,1024]{1,0:T(8,128)(2,1)}, bf16[32,1024]{1,0:T(8,128)(2,1)}) custom-call(bf16[128,512]{1,0:T(8,128)(2,1)} %get-tuple-element.255.refs_0_, bf16[128,512]{1,0:T(8,128)(2,1)} %copy-done.12, bf16[128,512]{1,0:T(8,128)(2,1)} %get-tuple-element.256.refs_2_, ...), custom_call_target="tpu_custom_call" | custom-call | tf_op jit(solution)/shard_map/unpack_gradients/pallas_call | solution.py:284
  (119 shorter events, 17.1 us)
Async XLA Ops:
  2.6 6.7 %collective-permute-start = (bf16[128,512]{1,0:T(8,128)(2,1)}, bf16[128,512]{1,0:T(8,128)(2,1)S(1)}, u32[]{:S(2)}, u32[]{:S(2)}) collective-permute-start(bf16[128,512]{1,0:T(8,128)(2,1)} %get-tuple-element.105), channel_id=1, source_target_pairs={{0,1},{1,0},{2,3},{3,2},{4,5},{5,4},{6,7},{7,6},{8,9},{9,8},{10,11... | collective-permute-start | bytes 393224 | tf_op jit(solution)/shard_map/ppermute | solution.py:31
  9.4 6.0 %collective-permute-start.2 = (bf16[64,512]{1,0:T(8,128)(2,1)S(1)}, bf16[64,512]{1,0:T(8,128)(2,1)S(1)}, u32[]{:S(2)}, u32[]{:S(2)}) collective-permute-start(bf16[64,512]{1,0:T(8,128)(2,1)S(1)} %pad_maximum_fusion.4), channel_id=1, source_target_pairs={{0,8},{2,10},{4,12},{6,14},{8,0},{10,2},{12,4},{14,6},{16,24},{18,... | collective-permute-start | bytes 196616 | tf_op jit(solution)/shard_map/ppermute | solution.py:26
  11.2 8.4 %collective-permute-start.4 = (bf16[64,512]{1,0:T(8,128)(2,1)S(1)}, bf16[64,512]{1,0:T(8,128)(2,1)S(1)}, u32[]{:S(2)}, u32[]{:S(2)}) collective-permute-start(bf16[64,512]{1,0:T(8,128)(2,1)S(1)} %pad_maximum_fusion.4), channel_id=1, source_target_pairs={{0,24},{2,26},{4,28},{6,30},{8,16},{10,18},{12,20},{14,22},{16,8},... | collective-permute-start | bytes 196616 | tf_op jit(solution)/shard_map/ppermute | solution.py:26
  13.7 5.9 %collective-permute-start.3 = (bf16[64,512]{1,0:T(8,128)(2,1)S(1)}, bf16[64,512]{1,0:T(8,128)(2,1)S(1)}, u32[]{:S(2)}, u32[]{:S(2)}) collective-permute-start(bf16[64,512]{1,0:T(8,128)(2,1)S(1)} %pad_maximum_fusion.4), channel_id=1, source_target_pairs={{0,16},{2,18},{4,20},{6,22},{8,24},{10,26},{12,28},{14,30},{16,0},... | collective-permute-start | bytes 196616 | tf_op jit(solution)/shard_map/ppermute | solution.py:26
  13.8 7.5 %collective-permute-start.1 = (bf16[192,768]{1,0:T(8,128)(2,1)}, bf16[192,768]{1,0:T(8,128)(2,1)S(1)}, u32[]{:S(2)}, u32[]{:S(2)}) collective-permute-start(bf16[192,768]{1,0:T(8,128)(2,1)} %get-tuple-element.107), channel_id=1, source_target_pairs={{0,1},{1,0},{2,3},{3,2},{4,5},{5,4},{6,7},{7,6},{8,9},{9,8},{10,11... | collective-permute-start | bytes 884744 | tf_op jit(solution)/shard_map/ppermute | solution.py:31
  19.6 6.7 %collective-permute-start.6 = (bf16[256,512]{1,0:T(8,128)(2,1)S(1)}, bf16[256,512]{1,0:T(8,128)(2,1)S(1)}, u32[]{:S(2)}, u32[]{:S(2)}) collective-permute-start(bf16[256,512]{1,0:T(8,128)(2,1)S(1)} %get-tuple-element.246), channel_id=1, source_target_pairs={{0,4},{2,6},{4,0},{6,2},{8,12},{10,14},{12,8},{14,10},{16,20},{18,... | collective-permute-start | bytes 786440 | tf_op jit(solution)/shard_map/ppermute | solution.py:26
  21.4 5.0 %collective-permute-start.5 = (bf16[128,512]{1,0:T(8,128)(2,1)S(1)}, bf16[128,512]{1,0:T(8,128)(2,1)S(1)}, u32[]{:S(2)}, u32[]{:S(2)}) collective-permute-start(bf16[128,512]{1,0:T(8,128)(2,1)S(1)} %copy-done.17), channel_id=1, source_target_pairs={{0,1},{1,0},{2,3},{3,2},{4,5},{5,4},{6,7},{7,6},{8,9},{9,8},{10,11... | collective-permute-start | bytes 393224 | tf_op jit(solution)/shard_map/ppermute | solution.py:31
  26.4 12.8 %collective-permute-start.12 = (bf16[192,768]{1,0:T(8,128)(2,1)S(1)}, bf16[192,768]{1,0:T(8,128)(2,1)S(1)}, u32[]{:S(2)}, u32[]{:S(2)}) collective-permute-start(bf16[192,768]{1,0:T(8,128)(2,1)S(1)} %copy-done.16), channel_id=1, source_target_pairs={{0,1},{1,0},{2,3},{3,2},{4,5},{5,4},{6,7},{7,6},{8,9},{9,8},{10,11... | collective-permute-start | bytes 884744 | tf_op jit(solution)/shard_map/ppermute | solution.py:31
  28.0 11.2 %collective-permute-start.11 = (bf16[192,768]{1,0:T(8,128)(2,1)S(1)}, bf16[192,768]{1,0:T(8,128)(2,1)S(1)}, u32[]{:S(2)}, u32[]{:S(2)}) collective-permute-start(bf16[192,768]{1,0:T(8,128)(2,1)S(1)} %copy-done.15), channel_id=1, source_target_pairs={{0,1},{1,0},{2,3},{3,2},{4,5},{5,4},{6,7},{7,6},{8,9},{9,8},{10,11... | collective-permute-start | bytes 884744 | tf_op jit(solution)/shard_map/ppermute | solution.py:31
  28.5 4.3 %collective-permute-start.7 = (bf16[704,512]{1,0:T(8,128)(2,1)S(1)}, bf16[704,512]{1,0:T(8,128)(2,1)S(1)}, u32[]{:S(2)}, u32[]{:S(2)}) collective-permute-start(bf16[704,512]{1,0:T(8,128)(2,1)S(1)} %constant_dynamic-update-slice_fusion.5.refs_1_), channel_id=1, source_target_pairs={{0,2},{2,0},{4,6},{6,4},{8,10},{10,8},{12,14},{14,12},{16,18},{18,... | collective-permute-start | bytes 2162696 | tf_op jit(solution)/shard_map/ppermute | solution.py:26
  28.6 10.1 %collective-permute-start.10 = (bf16[64,512]{1,0:T(8,128)(2,1)S(1)}, bf16[64,512]{1,0:T(8,128)(2,1)S(1)}, u32[]{:S(2)}, u32[]{:S(2)}) collective-permute-start(bf16[64,512]{1,0:T(8,128)(2,1)S(1)} %pad_maximum_fusion.5), channel_id=1, source_target_pairs={{0,24},{2,26},{4,28},{6,30},{8,16},{10,18},{12,20},{14,22},{16,8},... | collective-permute-start | bytes 196616 | tf_op jit(solution)/shard_map/ppermute | solution.py:26
  31.2 7.9 %collective-permute-start.9 = (bf16[64,512]{1,0:T(8,128)(2,1)S(1)}, bf16[64,512]{1,0:T(8,128)(2,1)S(1)}, u32[]{:S(2)}, u32[]{:S(2)}) collective-permute-start(bf16[64,512]{1,0:T(8,128)(2,1)S(1)} %pad_maximum_fusion.5), channel_id=1, source_target_pairs={{0,16},{2,18},{4,20},{6,22},{8,24},{10,26},{12,28},{14,30},{16,0},... | collective-permute-start | bytes 196616 | tf_op jit(solution)/shard_map/ppermute | solution.py:26
  32.8 6.4 %collective-permute-start.8 = (bf16[64,512]{1,0:T(8,128)(2,1)S(1)}, bf16[64,512]{1,0:T(8,128)(2,1)S(1)}, u32[]{:S(2)}, u32[]{:S(2)}) collective-permute-start(bf16[64,512]{1,0:T(8,128)(2,1)S(1)} %pad_maximum_fusion.5), channel_id=1, source_target_pairs={{0,8},{2,10},{4,12},{6,14},{8,0},{10,2},{12,4},{14,6},{16,24},{18,... | collective-permute-start | bytes 196616 | tf_op jit(solution)/shard_map/ppermute | solution.py:26
  39.3 8.5 %collective-permute-start.14 = (bf16[256,512]{1,0:T(8,128)(2,1)S(1)}, bf16[256,512]{1,0:T(8,128)(2,1)S(1)}, u32[]{:S(2)}, u32[]{:S(2)}) collective-permute-start(bf16[256,512]{1,0:T(8,128)(2,1)S(1)} %get-tuple-element.240), channel_id=1, source_target_pairs={{0,4},{2,6},{4,0},{6,2},{8,12},{10,14},{12,8},{14,10},{16,20},{18,... | collective-permute-start | bytes 786440 | tf_op jit(solution)/shard_map/ppermute | solution.py:26
  40.8 8.7 %collective-permute-start.13 = (bf16[192,768]{1,0:T(8,128)(2,1)S(1)}, bf16[192,768]{1,0:T(8,128)(2,1)S(1)}, u32[]{:S(2)}, u32[]{:S(2)}) collective-permute-start(bf16[192,768]{1,0:T(8,128)(2,1)S(1)} %copy-done.14), channel_id=1, source_target_pairs={{0,1},{1,0},{2,3},{3,2},{4,5},{5,4},{6,7},{7,6},{8,9},{9,8},{10,11... | collective-permute-start | bytes 884744 | tf_op jit(solution)/shard_map/ppermute | solution.py:31
  47.8 3.3 %collective-permute-start.15 = (bf16[704,512]{1,0:T(8,128)(2,1)S(1)}, bf16[704,512]{1,0:T(8,128)(2,1)S(1)}, u32[]{:S(2)}, u32[]{:S(2)}) collective-permute-start(bf16[704,512]{1,0:T(8,128)(2,1)S(1)} %constant_dynamic-update-slice_fusion.16.refs_1_), channel_id=1, source_target_pairs={{0,2},{2,0},{4,6},{6,4},{8,10},{10,8},{12,14},{14,12},{16,18},{18,... | collective-permute-start | bytes 2162696 | tf_op jit(solution)/shard_map/ppermute | solution.py:26
  49.5 7.5 %collective-permute-start.16 = (bf16[704,512]{1,0:T(8,128)(2,1)S(1)}, bf16[704,512]{1,0:T(8,128)(2,1)S(1)}, u32[]{:S(2)}, u32[]{:S(2)}) collective-permute-start(bf16[704,512]{1,0:T(8,128)(2,1)S(1)} %get-tuple-element.152), channel_id=1, source_target_pairs={{0,2},{2,0},{4,6},{6,4},{8,10},{10,8},{12,14},{14,12},{16,18},{18,... | collective-permute-start | bytes 2162696 | tf_op jit(solution)/shard_map/ppermute | solution.py:26
  49.5 9.4 %collective-permute-start.17 = (bf16[192,768]{1,0:T(8,128)(2,1)S(1)}, bf16[192,768]{1,0:T(8,128)(2,1)S(1)}, u32[]{:S(2)}, u32[]{:S(2)}) collective-permute-start(bf16[192,768]{1,0:T(8,128)(2,1)S(1)} %get-tuple-element.164), channel_id=1, source_target_pairs={{0,1},{1,0},{2,3},{3,2},{4,5},{5,4},{6,7},{7,6},{8,9},{9,8},{10,11... | collective-permute-start | bytes 884744 | tf_op jit(solution)/shard_map/ppermute | solution.py:31
  56.4 9.2 %collective-permute-start.19 = (bf16[192,768]{1,0:T(8,128)(2,1)S(1)}, bf16[192,768]{1,0:T(8,128)(2,1)S(1)}, u32[]{:S(2)}, u32[]{:S(2)}) collective-permute-start(bf16[192,768]{1,0:T(8,128)(2,1)S(1)} %get-tuple-element.174), channel_id=1, source_target_pairs={{0,1},{1,0},{2,3},{3,2},{4,5},{5,4},{6,7},{7,6},{8,9},{9,8},{10,11... | collective-permute-start | bytes 884744 | tf_op jit(solution)/shard_map/ppermute | solution.py:31
  57.3 8.2 %collective-permute-start.18 = (bf16[256,512]{1,0:T(8,128)(2,1)S(1)}, bf16[256,512]{1,0:T(8,128)(2,1)S(1)}, u32[]{:S(2)}, u32[]{:S(2)}) collective-permute-start(bf16[256,512]{1,0:T(8,128)(2,1)S(1)} %slice.223), channel_id=1, source_target_pairs={{0,4},{2,6},{4,0},{6,2},{8,12},{10,14},{12,8},{14,10},{16,20},{18,... | collective-permute-start | bytes 786440 | tf_op jit(solution)/shard_map/ppermute | solution.py:26
  66.4 2.6 %collective-permute-start.20 = (bf16[704,512]{1,0:T(8,128)(2,1)S(1)}, bf16[704,512]{1,0:T(8,128)(2,1)S(1)}, u32[]{:S(2)}, u32[]{:S(2)}) collective-permute-start(bf16[704,512]{1,0:T(8,128)(2,1)S(1)} %get-tuple-element.176), channel_id=1, source_target_pairs={{0,2},{2,0},{4,6},{6,4},{8,10},{10,8},{12,14},{14,12},{16,18},{18,... | collective-permute-start | bytes 2162696 | tf_op jit(solution)/shard_map/ppermute | solution.py:26
  66.4 22.4 %collective-permute-start.28 = (bf16[192,768]{1,0:T(8,128)(2,1)S(1)}, bf16[192,768]{1,0:T(8,128)(2,1)S(1)}, u32[]{:S(2)}, u32[]{:S(2)}) collective-permute-start(bf16[192,768]{1,0:T(8,128)(2,1)S(1)} %get-tuple-element.184), channel_id=1, source_target_pairs={{0,1},{1,0},{2,3},{3,2},{4,5},{5,4},{6,7},{7,6},{8,9},{9,8},{10,11... | collective-permute-start | bytes 884744 | tf_op jit(solution)/shard_map/ppermute | solution.py:31
  69.3 9.5 %collective-permute-start.21 = (bf16[256,512]{1,0:T(8,128)(2,1)S(1)}, bf16[256,512]{1,0:T(8,128)(2,1)S(1)}, u32[]{:S(2)}, u32[]{:S(2)}) collective-permute-start(bf16[256,512]{1,0:T(8,128)(2,1)S(1)} %slice.171), channel_id=1, source_target_pairs={{0,4},{2,6},{4,0},{6,2},{8,12},{10,14},{12,8},{14,10},{16,20},{18,... | collective-permute-start | bytes 786440 | tf_op jit(solution)/shard_map/ppermute | solution.py:26
  70.2 6.5 %collective-permute-start.24 = (bf16[64,512]{1,0:T(8,128)(2,1)S(1)}, bf16[64,512]{1,0:T(8,128)(2,1)S(1)}, u32[]{:S(2)}, u32[]{:S(2)}) collective-permute-start(bf16[64,512]{1,0:T(8,128)(2,1)S(1)} %get-tuple-element.219), channel_id=1, source_target_pairs={{0,24},{2,26},{4,28},{6,30},{8,16},{10,18},{12,20},{14,22},{16,8},... | collective-permute-start | bytes 196616 | tf_op jit(solution)/shard_map/ppermute | solution.py:26
  73.0 5.8 %collective-permute-start.23 = (bf16[64,512]{1,0:T(8,128)(2,1)S(1)}, bf16[64,512]{1,0:T(8,128)(2,1)S(1)}, u32[]{:S(2)}, u32[]{:S(2)}) collective-permute-start(bf16[64,512]{1,0:T(8,128)(2,1)S(1)} %get-tuple-element.220), channel_id=1, source_target_pairs={{0,16},{2,18},{4,20},{6,22},{8,24},{10,26},{12,28},{14,30},{16,0},... | collective-permute-start | bytes 196616 | tf_op jit(solution)/shard_map/ppermute | solution.py:26
  73.0 5.8 %collective-permute-start.22 = (bf16[64,512]{1,0:T(8,128)(2,1)S(1)}, bf16[64,512]{1,0:T(8,128)(2,1)S(1)}, u32[]{:S(2)}, u32[]{:S(2)}) collective-permute-start(bf16[64,512]{1,0:T(8,128)(2,1)S(1)} %get-tuple-element.221), channel_id=1, source_target_pairs={{0,8},{2,10},{4,12},{6,14},{8,0},{10,2},{12,4},{14,6},{16,24},{18,... | collective-permute-start | bytes 196616 | tf_op jit(solution)/shard_map/ppermute | solution.py:26
  76.8 12.1 %collective-permute-start.29 = (bf16[192,768]{1,0:T(8,128)(2,1)S(1)}, bf16[192,768]{1,0:T(8,128)(2,1)S(1)}, u32[]{:S(2)}, u32[]{:S(2)}) collective-permute-start(bf16[192,768]{1,0:T(8,128)(2,1)S(1)} %get-tuple-element.185), channel_id=1, source_target_pairs={{0,1},{1,0},{2,3},{3,2},{4,5},{5,4},{6,7},{7,6},{8,9},{9,8},{10,11... | collective-permute-start | bytes 884744 | tf_op jit(solution)/shard_map/ppermute | solution.py:31
  79.0 5.0 %collective-permute-start.25 = (bf16[64,512]{1,0:T(8,128)(2,1)S(1)}, bf16[64,512]{1,0:T(8,128)(2,1)S(1)}, u32[]{:S(2)}, u32[]{:S(2)}) collective-permute-start(bf16[64,512]{1,0:T(8,128)(2,1)S(1)} %get-tuple-element.216), channel_id=1, source_target_pairs={{0,8},{2,10},{4,12},{6,14},{8,0},{10,2},{12,4},{14,6},{16,24},{18,... | collective-permute-start | bytes 196616 | tf_op jit(solution)/shard_map/ppermute | solution.py:26
  80.0 6.5 %collective-permute-start.27 = (bf16[64,512]{1,0:T(8,128)(2,1)S(1)}, bf16[64,512]{1,0:T(8,128)(2,1)S(1)}, u32[]{:S(2)}, u32[]{:S(2)}) collective-permute-start(bf16[64,512]{1,0:T(8,128)(2,1)S(1)} %get-tuple-element.217), channel_id=1, source_target_pairs={{0,24},{2,26},{4,28},{6,30},{8,16},{10,18},{12,20},{14,22},{16,8},... | collective-permute-start | bytes 196616 | tf_op jit(solution)/shard_map/ppermute | solution.py:26
  81.9 6.9 %collective-permute-start.26 = (bf16[64,512]{1,0:T(8,128)(2,1)S(1)}, bf16[64,512]{1,0:T(8,128)(2,1)S(1)}, u32[]{:S(2)}, u32[]{:S(2)}) collective-permute-start(bf16[64,512]{1,0:T(8,128)(2,1)S(1)} %get-tuple-element.218), channel_id=1, source_target_pairs={{0,16},{2,18},{4,20},{6,22},{8,24},{10,26},{12,28},{14,30},{16,0},... | collective-permute-start | bytes 196616 | tf_op jit(solution)/shard_map/ppermute | solution.py:26
  84.1 8.0 %collective-permute-start.30 = (bf16[128,512]{1,0:T(8,128)(2,1)S(1)}, bf16[128,512]{1,0:T(8,128)(2,1)S(1)}, u32[]{:S(2)}, u32[]{:S(2)}) collective-permute-start(bf16[128,512]{1,0:T(8,128)(2,1)S(1)} %pad_maximum_fusion.1), channel_id=1, source_target_pairs={{0,1},{1,0},{2,3},{3,2},{4,5},{5,4},{6,7},{7,6},{8,9},{9,8},{10,11... | collective-permute-start | bytes 393224 | tf_op jit(solution)/shard_map/ppermute | solution.py:31
  88.9 5.2 %collective-permute-start.31 = (bf16[128,512]{1,0:T(8,128)(2,1)S(1)}, bf16[128,512]{1,0:T(8,128)(2,1)S(1)}, u32[]{:S(2)}, u32[]{:S(2)}) collective-permute-start(bf16[128,512]{1,0:T(8,128)(2,1)S(1)} %pad_maximum_fusion.3), channel_id=1, source_target_pairs={{0,1},{1,0},{2,3},{3,2},{4,5},{5,4},{6,7},{7,6},{8,9},{9,8},{10,11... | collective-permute-start | bytes 393224 | tf_op jit(solution)/shard_map/ppermute | solution.py:31
  (18 other events, 168.7 us)
